TPU v7x, 32 devices: a whole 2x2x4 slice. The times are simulated.
32 devices in a mesh: energy: 8 (over z, x), mom: 4 (over y, core).
Axes of the slice: x: 2, y: 2, z: 4, core: 2. Of those that a mesh axis runs over, the one named last changes fastest.
Arguments:
- green_less: float32 [4, 8, 8, 64, 128], P('mom', 'energy'), may hold values from -6 to 6
- couplings: bfloat16 [32, 3, 64, 64], replicated, may hold values from -0.75 to 0.75
- pair_atoms: int32 [8, 2], replicated, may hold values from 0 to 31
- shift_idx: int32 [3], replicated, may hold values from 1 to 4, as said below
- weights: float32 [2, 3, 4], replicated, may hold values from 0.05 to 1
Outputs:
- sigma_less: float32 [4, 8, 8, 64, 128], P('mom', 'energy')
Inputs may be any that keep to these rules, and one draw needn't show every extreme that they name: `shift_idx`: one mode's shift is exactly 4 and another's is exactly 1.
All inputs are finite; a program needn't handle non-finite values.
Results may differ from a plain program's by a relative error of at most 0.0003.
Values sent between devices are 32-bit elements; how exact they have to be, the bound alone decides.
A program may use at most 64 MiB of HBM per device.

v0:
```python
import jax
import jax.numpy as jnp
from jax import lax
from jax.sharding import PartitionSpec as P

NMODE = 3


precise = lax.Precision.HIGHEST


def mixing_block(weights, target_ids, source_ids):
    moments = weights.shape[2]
    offset = (target_ids[:, None] - source_ids[None, :]) % moments
    selector = (offset[:, :, None] == jnp.arange(moments, dtype=jnp.int32)[None, None, :]).astype(
        jnp.float32
    )
    return jnp.einsum("slm,tjm->sltj", weights, selector, precision=precise)


def energy_operator(weights, shift_idx, target_ids, source_ids, energies):
    mixing = mixing_block(weights, target_ids, source_ids)
    energy_ids = jnp.arange(energies, dtype=jnp.int32)
    distance = energy_ids[None, :, None] - energy_ids[None, None, :]
    shifts = shift_idx[:, None, None]
    below_mask = (distance == shifts).astype(jnp.float32)
    above_mask = (distance == -shifts).astype(jnp.float32)
    below_part = mixing[0][:, :, None, :, None] * below_mask[:, None, :, None, :]
    above_part = mixing[1][:, :, None, :, None] * above_mask[:, None, :, None, :]
    return below_part + above_part


def apply_operator(operator, green_piece):
    sources = green_piece.shape[0]
    energies = green_piece.shape[1]
    flat = green_piece.reshape(sources, energies, -1)
    return jnp.einsum("ltejf,jfx->ltex", operator, flat, precision=precise)


def contract(mixed_flat, left_table, right_blocks, pair_dev, orbitals):
    mode_count = mixed_flat.shape[0]
    targets = mixed_flat.shape[1]
    energies = mixed_flat.shape[2]
    mixed = mixed_flat.reshape(mode_count, targets, energies, pair_dev, orbitals, 2 * orbitals)
    right_product = jnp.einsum("ltepac,lpcd->ltepad", mixed, right_blocks, precision=precise)
    return jnp.einsum("lpab,ltepbd->tepad", left_table, right_product, precision=precise)


def pair_couplings(couplings, atom_ids):
    atom_count = couplings.shape[0]
    orbitals = couplings.shape[2]
    onehot = (atom_ids[:, None] == jnp.arange(atom_count, dtype=jnp.int32)[None, :]).astype(
        jnp.bfloat16
    )
    selected = jnp.dot(
        onehot, couplings.reshape(atom_count, -1), preferred_element_type=jnp.float32
    )
    return selected.reshape(atom_ids.shape[0], NMODE, orbitals, orbitals).transpose(1, 0, 2, 3)


def block_diagonal(right_table):
    orbitals = right_table.shape[2]
    identity = jnp.eye(2, dtype=jnp.float32)
    blocks = jnp.einsum("qr,lpdc->lpqcrd", identity, right_table, precision=precise)
    return blocks.reshape(right_table.shape[0], right_table.shape[1], 2 * orbitals, 2 * orbitals)


def on_device(green_less, couplings, pair_atoms, shift_idx, weights):
    relaid = lax.all_to_all(green_less, "energy", split_axis=2, concat_axis=1, tiled=True)
    mom_dev = relaid.shape[0]
    energies = relaid.shape[1]
    pair_dev = relaid.shape[2]
    orbitals = relaid.shape[3]
    pair_start = lax.axis_index("energy") * pair_dev
    local_atoms = lax.dynamic_slice_in_dim(pair_atoms, pair_start, pair_dev, 0)
    left_table = pair_couplings(couplings, local_atoms[:, 0])
    right_blocks = block_diagonal(pair_couplings(couplings, local_atoms[:, 1]))
    own_moms = lax.axis_index("mom") * mom_dev + jnp.arange(mom_dev, dtype=jnp.int32)
    shard_piece = lax.all_gather(relaid, "mom", axis=0, tiled=True)
    source_ids = jnp.arange(shard_piece.shape[0], dtype=jnp.int32)
    operator = energy_operator(weights, shift_idx, own_moms, source_ids, energies)
    mixed_all = apply_operator(operator, shard_piece)
    result = contract(mixed_all, left_table, right_blocks, pair_dev, orbitals)
    return lax.all_to_all(result, "energy", split_axis=1, concat_axis=2, tiled=True)


def solution(mesh):
    return jax.shard_map(
        on_device,
        mesh=mesh,
        in_specs=(P("mom", "energy", None, None, None), P(), P(), P(), P()),
        out_specs=P("mom", "energy", None, None, None),
        check_vma=False,
    )
```

profile of v0, /device:TPU:0, one launch (start us, length us, event | category | flops | bytes accessed | tf_op | source)
XLA Modules:
  0.0 66.6 jit_solution(2758992086051350166)
XLA Ops:
  6.5 0.0 copy-start
  6.5 7.4 %all-to-all-start = ((f32[1,1,8,64,128]{4,3,1,0,2:T(8,128)}), f32[1,1,8,64,128]{4,3,1,0,2:T(8,128)S(1)}, u32[]{:S(2)}, u32[]{:S(2)}) async-start(f32[1,1,8,64,128]{4,3,1,0,2:T(8,128)} %bitcast.85), calls=%async_computation | async-start | bytes 524288 | tf_op jit(solution)/shard_map/all_to_all | solution.py:69
  13.9 0.0 all-gather.3.cloned.1.call-start
  14.0 0.0 copy-done
  14.0 0.2 convolution_bitcast_fusion.2
  14.2 8.7 %all-to-all-done = f32[1,1,8,64,128]{4,3,1,0,2:T(8,128)S(1)} async-done(((f32[1,1,8,64,128]{4,3,1,0,2:T(8,128)}), f32[1,1,8,64,128]{4,3,1,0,2:T(8,128)S(1)}, u32[]{:S(2)}, u32[]{:S(2)}) %all-to-all-start) | async-done | bytes 262176 | tf_op jit(solution)/shard_map/all_to_all | solution.py:69
  22.8 0.0 copy-start.1
  22.8 0.7 %copy-done.1 = f32[1,1,8,64,128]{4,3,1,0,2:T(8,128)} copy-done((f32[1,1,8,64,128]{4,3,1,0,2:T(8,128)}, f32[1,1,8,64,128]{4,3,1,0,2:T(8,128)S(1)}, u32[]{:S(2)}) %copy-start.1) | copy-done | bytes 262168
  23.5 0.0 all-gather.3.cloned.1.call-update
  23.6 0.7 neg.4
  24.2 0.7 %compare_convert_fusion.1 = (f32[3,8,8]{2,1,0:T(8,128)S(1)}, f32[3,8,8]{2,1,0:T(8,128)S(1)}) fusion(s32[8,8]{1,0:T(8,128)S(1)} %iota_subtract_fusion, s32[3]{0:T(128)} %param.8, s32[3]{0:T(128)S(1)} %neg.4), kind=kLoop, calls=%fused_computation.15 | loop fusion | flops 768 | bytes 1816 | tf_op jit(solution)/shard_map/convert_element_type | solution.py:26
  25.0 0.1 add_bitcast_fusion
  25.1 0.2 copy.16
  25.3 2.4 %reshape.178 = bf16[32,12288]{1,0:T(8,128)(2,1)S(1)} reshape(bf16[32,3,64,64]{3,2,1,0:T(8,128)(2,1)} %param.6) | data formatting | bytes 1572864 | tf_op jit(solution)/shard_map/reshape | solution.py:56
  27.8 0.0 copy-start.2
  27.8 1.7 %reshape.179 = bf16[3,64,64,32]{2,1,0,3:T(8,128)(2,1)S(1)} reshape(bf16[12288,32]{0,1:T(8,128)(2,1)S(1)} %bitcast.80) | data formatting | bytes 1572864 | tf_op jit(solution)/shard_map/reshape.87
  29.5 0.0 copy-done.2
  29.5 0.1 constant_dynamic-slice_fusion
  29.6 0.5 fusion.22
  30.1 1.5 %fusion.2 = f32[1,3,64,64]{3,0,2,1:T(1,128)S(1)} fusion(bf16[3,64,64,32]{2,1,0,3:T(8,128)(2,1)S(1)} %reshape.179, s32[]{:T(128)} %bitcast), kind=kOutput, calls=%fused_computation.2 | convolution fusion | flops 786464 | bytes 835588 | tf_op jit(solution)/shard_map/dot_general | solution.py:55
  31.7 0.1 copy.15
  31.8 0.2 multiply_bitcast_fusion
  31.9 0.2 reshape.192
  32.2 1.6 %fusion = f32[1,3,64,64]{3,0,2,1:T(1,128)S(1)} fusion(bf16[3,64,64,32]{2,1,0,3:T(8,128)(2,1)S(1)} %reshape.179, s32[]{:T(128)} %bitcast.23), kind=kOutput, calls=%fused_computation | convolution fusion | flops 786464 | bytes 835588 | tf_op jit(solution)/shard_map/dot_general | solution.py:55
  33.8 5.7 %all-gather.3.cloned.1.call-done = f32[4,1,8,64,128]{4,3,2,1,0:T(8,128)} async-done(((f32[1,1,8,64,128]{4,3,2,1,0:T(8,128)}), f32[4,1,8,64,128]{4,3,2,1,0:T(8,128)}) %all-gather.3.cloned.1.call-update) | async-done | bytes 1048592 | tf_op jit(solution)/shard_map/all_gather | solution.py:79
  39.5 1.4 %reshape.181 = f32[4,8,8192]{2,1,0:T(8,128)S(1)} reshape(f32[4,1,8,64,128]{4,3,2,1,0:T(8,128)} %all-gather.3.cloned.1.call-done) | data formatting | bytes 2097152 | tf_op jit(solution)/shard_map/reshape | solution.py:36
  40.9 2.1 %fusion.4 = f32[3,8,64,128,1]{3,1,4,2,0:T(8,128)S(1)} fusion(f32[3,8,8,4,1]{2,1,3,4,0:T(8,128)S(1)} %copy.16, f32[4,8,8192]{2,1,0:T(8,128)S(1)} %reshape.181), kind=kOutput, calls=%fused_computation.7 | convolution fusion | flops 75497472 | bytes 1838080 | tf_op jit(solution)/shard_map/ltejf,jfx->ltex/dot_general | solution.py:37
  43.0 0.9 %convolution_bitcast_fusion = f32[3,8,64,128]{3,2,1,0:T(8,128)S(1)} fusion(f32[3,8,64,128,1]{3,1,4,2,0:T(8,128)S(1)} %fusion.4, f32[3,128,128,1]{2,1,0,3:T(8,128)S(1)} %reshape.192), kind=kOutput, calls=%fused_computation.4 | convolution fusion | flops 301989888 | bytes 1769472 | tf_op jit(solution)/shard_map/ltepac,lpcd->ltepad/dot_general | solution.py:45
  43.8 0.6 convolution_bitcast_fusion.1
  44.5 14.6 %all_to_all.24 = f32[1,8,1,64,128]{4,3,0,2,1:T(8,128)S(1)} all-to-all(f32[1,8,1,64,128]{4,3,0,2,1:T(8,128)S(1)} %convolution_bitcast_fusion.1), channel_id=1, replica_groups=mesh['energy'=8,'mom'=4] {'energy'}, dimensions={1} | all-to-all | bytes 524288 | tf_op jit(solution)/shard_map/all_to_all | solution.py:84
  59.1 0.7 %copy.37 = f32[1,1,8,64,128]{4,3,2,1,0:T(8,128)} copy(f32[1,1,8,64,128]{4,3,2,1,0:T(8,128)S(1)} %bitcast.82) | data formatting | bytes 524288
  (4 shorter events, 0.0 us)
Async XLA Ops:
  6.5 7.5 %copy-start = (f32[2,3,4]{2,0,1:T(2,128)S(1)}, f32[2,3,4]{2,0,1:T(2,128)}, u32[]{:S(2)}) copy-start(f32[2,3,4]{2,0,1:T(2,128)} %param.9) | copy-start | bytes 292
  6.5 16.3 %all-to-all-start = ((f32[1,1,8,64,128]{4,3,1,0,2:T(8,128)}), f32[1,1,8,64,128]{4,3,1,0,2:T(8,128)S(1)}, u32[]{:S(2)}, u32[]{:S(2)}) async-start(f32[1,1,8,64,128]{4,3,1,0,2:T(8,128)} %bitcast.85), calls=%async_computation | async-start | bytes 524288 | tf_op jit(solution)/shard_map/all_to_all | solution.py:69
  13.9 25.6 %all-gather.3.cloned.1.call-start = ((), (), s32[]{:S(2)}) async-start(), calls=%async_computation.2 | async-start | bytes 1310720 | tf_op jit(solution)/shard_map/all_gather | solution.py:79
  22.8 0.7 %copy-start.1 = (f32[1,1,8,64,128]{4,3,1,0,2:T(8,128)}, f32[1,1,8,64,128]{4,3,1,0,2:T(8,128)S(1)}, u32[]{:S(2)}) copy-start(f32[1,1,8,64,128]{4,3,1,0,2:T(8,128)S(1)} %all-to-all-done) | copy-start | bytes 786436
  27.8 1.8 %copy-start.2 = (s32[8,2]{0,1:T(2,128)S(1)}, s32[8,2]{0,1:T(2,128)}, u32[]{:S(2)}) copy-start(s32[8,2]{0,1:T(2,128)} %param.7) | copy-start | bytes 196
Sparse Core Ops, SparseCore 0:
  23.7 15.7 all-gather.2
where the time goes:
time: 67 us; the launch traced here: 66.6 us
  blocking collectives  14.6 us (22%)
  waiting for transfers between devices  14.4 us (21%)
  between operations  13.5 us (20%)
  local copies, waits for them, and re-layouts  8.17 us (12%)
  starting transfers between devices  7.42 us (11%)
  matrix products  6.85 us (10%)
  other arithmetic  1.7 us (3%)
    all_to_all x1, blocking collectives, on_device(): lax.all_to_all(result, 'energy', split_axis=1, concat_axis=2, tiled=True)  14.6 us
    all_to_all x1, waiting for transfers between devices, on_device(): lax.all_to_all(green_less, 'energy', split_axis=2, concat_axis=1, tiled=T...  8.65 us
    all_to_all x1, starting transfers between devices, on_device(): lax.all_to_all(green_less, 'energy', split_axis=2, concat_axis=1, tiled=T...  7.38 us
    all_gather x1, waiting for transfers between devices, on_device(): shard_piece = lax.all_gather(relaid, 'mom', axis=0, tiled=True)  5.7 us
    dot_general x2, matrix products, pair_couplings(): jnp.dot(onehot, couplings.reshape(atom_count, -1), preferred_element_type...  3.12 us
    reshape x1, local copies, waits for them, and re-layouts, pair_couplings(): couplings.reshape(atom_count, -1)  2.43 us
    dot_general x1, matrix products, apply_operator(): return jnp.einsum('ltejf,jfx->ltex', operator, flat, precision=precise)  2.05 us
    another operation x2, local copies, waits for them, and re-layouts  1.97 us
  transfers between devices with their start and end apart: 2, of which 2 were waited for; matrix products, arithmetic and copies ran while one was open for 16% of the time, Pallas kernels for 0%

commit v1 on v0

v1 whole, which is shorter than its diff:
```python
import functools

import jax
import jax.numpy as jnp
from jax import lax
from jax.experimental import pallas as pl
from jax.experimental.pallas import tpu as pltpu
from jax.sharding import PartitionSpec as P

HALVES = 2
SHIFT_MAX = 4
MESH = pl.DeviceIdType.MESH


def split(value):
    high = value.astype(jnp.bfloat16)
    return high, (value - high.astype(jnp.float32)).astype(jnp.bfloat16)


def left_lanes(shape):
    return lax.broadcasted_iota(jnp.int32, shape, len(shape) - 1) < shape[-1] // 2


def iota(shape, axis):
    return lax.broadcasted_iota(jnp.int32, shape, axis)


def kernel(
    sizes,
    green_hbm, couplings_hbm, pair_atoms, shift_idx, weights,
    out_ref,
    green, couplings, packed, held, result, landed, left_table, right_table,
    load_sem, in_send, in_recv, side_send, side_recv, out_send, out_recv,
):
    moms, energies, modes, orbitals, group = sizes
    lanes = 2 * orbitals
    rows = orbitals // 2
    cores = moms // HALVES
    here = lax.axis_index("energy")
    mom = lax.axis_index("mom")
    half, core = mom // cores, mom % cores

    def device(at, half_at, core_at):
        return (at, half_at * cores + core_at)

    def around(base, step, size):
        return lax.rem(base + step, size)

    barrier = pltpu.get_barrier_semaphore()
    for turn in range(HALVES):
        for step in range(1 if turn == 0 else 0, energies):
            pl.semaphore_signal(
                barrier, inc=1,
                device_id=device(around(here, step, energies), around(half, turn, HALVES), core),
                device_id_type=MESH,
            )
    for turn in range(1, cores):
        pl.semaphore_signal(
            barrier, inc=1, device_id=device(here, half, around(core, turn, cores)), device_id_type=MESH
        )

    load_green = pltpu.make_async_copy(green_hbm, green, load_sem.at[0])
    load_green.start()
    load_couplings = pltpu.make_async_copy(couplings_hbm, couplings, load_sem.at[1])
    load_couplings.start()

    edge = jnp.zeros((SHIFT_MAX, rows, lanes), jnp.float32)
    for source in range(moms):
        held[source, pl.ds(0, SHIFT_MAX)] = edge
        held[source, pl.ds(SHIFT_MAX + energies, SHIFT_MAX)] = edge

    load_green.wait()
    mask = left_lanes((rows, lanes))
    for pair in range(energies):
        top = green[0, 0, pair, pl.ds(0, rows), :]
        bottom = green[0, 0, pair, pl.ds(rows, rows), :]
        packed[0, pair] = jnp.where(mask, top, pltpu.roll(bottom, orbitals, 1))
        packed[1, pair] = jnp.where(mask, pltpu.roll(top, orbitals, 1), bottom)

    pl.semaphore_wait(barrier, HALVES * energies - 1 + cores - 1)

    def send_in(turn, step):
        to_half, to = around(half, turn, HALVES), around(here, step, energies)
        return pltpu.make_async_remote_copy(
            src_ref=packed.at[to_half, to],
            dst_ref=held.at[mom, SHIFT_MAX + here],
            send_sem=in_send.at[turn, step],
            recv_sem=in_recv.at[turn, step],
            device_id=device(to, to_half, core),
            device_id_type=MESH,
        )

    def send_side(turn, step, side):
        source = around(half, turn, HALVES) * cores + core
        slot = SHIFT_MAX + around(here, energies - step, energies)
        return pltpu.make_async_remote_copy(
            src_ref=held.at[source, slot],
            dst_ref=held.at[source, slot],
            send_sem=side_send.at[side, turn, step],
            recv_sem=side_recv.at[side, turn, step],
            device_id=device(here, half, around(core, side, cores)),
            device_id_type=MESH,
        )

    far_first = sorted(range(energies), key=lambda step: -min(step, energies - step))
    slots = [(turn, step) for step in far_first for turn in range(HALVES)]
    near_first = slots[::-1]
    remote = [slot for slot in slots if slot != (0, 0)]
    for turn, step in remote:
        send_in(turn, step).start()

    held[mom, SHIFT_MAX + here] = packed[half, here]

    load_couplings.wait()
    atom_a = pair_atoms[here, 0]
    atom_b = pair_atoms[here, 1]
    pick_same = (iota((orbitals, lanes), 0) == iota((orbitals, lanes), 1) % orbitals).astype(jnp.bfloat16)
    pick_other = (
        iota((orbitals, lanes), 0) == (iota((orbitals, lanes), 1) + rows) % orbitals
    ).astype(jnp.bfloat16)
    upper = iota((orbitals, lanes), 0) < rows
    same_block = (iota((lanes, lanes), 0) < orbitals) == (iota((lanes, lanes), 1) < orbitals)
    for mode in range(modes):
        left = couplings[atom_a, mode]
        right = couplings[atom_b, mode]
        left_same = jnp.dot(left, pick_same, preferred_element_type=jnp.float32)
        left_other = jnp.dot(left, pick_other, preferred_element_type=jnp.float32)
        left_table[:, pl.ds(mode * lanes, lanes)] = jnp.where(upper, left_same, left_other).astype(jnp.bfloat16)
        wide = jnp.dot(right, pick_same, preferred_element_type=jnp.float32).astype(jnp.bfloat16)
        tall = jnp.concatenate([wide, wide], axis=0)
        diagonal = jnp.where(same_block, tall.astype(jnp.float32), 0.0).astype(jnp.bfloat16)
        right_table[mode] = jnp.concatenate([diagonal, diagonal], axis=1)

    for turn, step in near_first:
        if (turn, step) != (0, 0):
            send_in(turn, step).wait_recv()
        for side in range(1, cores):
            send_side(turn, step, side).start()
    for turn, step in near_first:
        for side in range(1, cores):
            send_side(turn, step, side).wait_recv()

    def send_out(to_half, to):
        turn = lax.rem(to_half - half + HALVES, HALVES)
        step = lax.rem(to - here + energies, energies)
        return pltpu.make_async_remote_copy(
            src_ref=result.at[to_half, to],
            dst_ref=landed.at[half, here],
            send_sem=out_send.at[turn, step],
            recv_sem=out_recv.at[turn, step],
            device_id=device(to, to_half, core),
            device_id_type=MESH,
        )

    def one_group(index, carry):
        first = lax.rem(here // group + 1 + index, energies // group) * group
        sums = [[] for _ in range(modes)]
        for member in range(group):
            energy = first + member
            for mode in range(modes):
                shift = shift_idx[mode]
                totals = [None] * HALVES
                for offset in range(moms):
                    source = lax.rem(core - offset + moms, moms)
                    for sign, slot in ((0, energy - shift), (1, energy + shift)):
                        value = held[source, SHIFT_MAX + slot]
                        for target in range(HALVES):
                            term = weights[sign, mode, (target * cores + offset) % moms] * value
                            totals[target] = term if totals[target] is None else totals[target] + term
                sums[mode].extend(totals)
        rights = []
        for mode in range(modes):
            high, low = split(jnp.concatenate(sums[mode], axis=0))
            rights.append(
                lax.dot_general(
                    jnp.concatenate([high, low], axis=1), right_table[mode],
                    (((1,), (1,)), ((), ())), preferred_element_type=jnp.float32,
                )
            )
        for member in range(group):
            columns = []
            for target in range(HALVES):
                start = (member * HALVES + target) * rows
                stack = []
                for mode in range(modes):
                    block = rights[mode][start:start + rows]
                    high, low = split(jnp.concatenate([block, pltpu.roll(block, orbitals, 1)], axis=0))
                    stack += [high, low]
                columns.append(jnp.concatenate(stack, axis=0))
            product = jnp.dot(
                left_table[...], jnp.concatenate(columns, axis=1), preferred_element_type=jnp.float32
            )
            energy = first + member
            for target in range(HALVES):
                both = product[:, target * lanes:(target + 1) * lanes]
                result[target, energy] = jnp.where(mask, both[:rows], both[rows:])
                own = jnp.logical_and(energy == here, half == target)

                @pl.when(jnp.logical_not(own))
                def _():
                    send_out(target, energy).start()

        return carry

    lax.fori_loop(0, energies // group, one_group, 0)
    landed[half, here] = result[half, here]

    for step in reversed(far_first):
        for turn in range(HALVES):
            if (turn, step) != (0, 0):
                send_out(around(half, turn, HALVES), around(here, step, energies)).wait_recv()
        pair = around(here, energies - step, energies)
        real, imag = landed[0, pair], landed[1, pair]
        out_ref[0, 0, pair, pl.ds(0, rows), :] = jnp.where(mask, real, pltpu.roll(imag, orbitals, 1))
        out_ref[0, 0, pair, pl.ds(rows, rows), :] = jnp.where(mask, pltpu.roll(real, orbitals, 1), imag)

    for turn, step in slots:
        if (turn, step) != (0, 0):
            send_in(turn, step).wait_send()
            send_out(around(half, turn, HALVES), around(here, step, energies)).wait_send()
        for side in range(1, cores):
            send_side(turn, step, side).wait_send()


def on_device(moms, energies, green_less, couplings, pair_atoms, shift_idx, weights):
    modes, orbitals = couplings.shape[1], couplings.shape[2]
    lanes, rows, cores = 2 * orbitals, orbitals // 2, moms // HALVES
    group = next(size for size in (4, 2, 1) if energies % size == 0)
    smem = pl.BlockSpec(memory_space=pltpu.SMEM)
    hbm = pl.BlockSpec(memory_space=pl.ANY)
    dma = pltpu.SemaphoreType.DMA
    return pl.pallas_call(
        functools.partial(kernel, (moms, energies, modes, orbitals, group)),
        out_shape=jax.ShapeDtypeStruct(green_less.shape, jnp.float32),
        in_specs=[hbm, hbm, smem, smem, smem],
        out_specs=pl.BlockSpec(memory_space=pltpu.VMEM),
        scratch_shapes=[
            pltpu.VMEM(green_less.shape, jnp.float32),
            pltpu.VMEM(couplings.shape, jnp.bfloat16),
            pltpu.VMEM((HALVES, energies, rows, lanes), jnp.float32),
            pltpu.VMEM((moms, energies + 2 * SHIFT_MAX, rows, lanes), jnp.float32),
            pltpu.VMEM((HALVES, energies, rows, lanes), jnp.float32),
            pltpu.VMEM((HALVES, energies, rows, lanes), jnp.float32),
            pltpu.VMEM((orbitals, modes * lanes), jnp.bfloat16),
            pltpu.VMEM((modes, lanes, 2 * lanes), jnp.bfloat16),
            dma((2,)),
            dma((HALVES, energies)),
            dma((HALVES, energies)),
            dma((cores, HALVES, energies)),
            dma((cores, HALVES, energies)),
            dma((HALVES, energies)),
            dma((HALVES, energies)),
        ],
        compiler_params=pltpu.CompilerParams(
            collective_id=0, has_side_effects=True, vmem_limit_bytes=40 * 2**20
        ),
    )(green_less, couplings, pair_atoms, shift_idx, weights)


def solution(mesh):
    spec = P("mom", "energy", None, None, None)
    return jax.shard_map(
        functools.partial(on_device, mesh.shape["mom"], mesh.shape["energy"]),
        mesh=mesh,
        in_specs=(spec, P(), P(), P(), P()),
        out_specs=spec,
        check_vma=False,
    )
```

time: 67 us -> 29.1 us (0.43)
  the two profiles are of different devices: /device:TPU:0 before, /device:TPU:11 now
where the time goes in v1:
time: 29.1 us; the launch traced here: 28.9 us
  Pallas kernels  23.7 us (81%)
  local copies, waits for them, and re-layouts  5.15 us (18%)
    pallas_call x1, Pallas kernels, on_device(): pl.pallas_call(functools.partial(kernel, (moms, energies, modes, orbitals...  23.7 us
    unnamed x9, local copies, waits for them, and re-layouts  5.15 us

profile of v1, /device:TPU:11, one launch (start us, length us, event | category | flops | bytes accessed | tf_op | source)
XLA Modules:
  0.0 28.9 jit_solution(3970904267514862176)
XLA Ops:
  0.0 0.8 %copy.6.pair_atoms = s32[8,2]{1,0:T(8,128)S(1)} copy(s32[8,2]{0,1:T(2,128)} %param.7) | data formatting | bytes 128 | tf_op args[2]
  0.8 0.7 %copy.7.weights = f32[2,3,4]{2,1,0:T(4,128)S(1)} copy(f32[2,3,4]{2,0,1:T(2,128)} %param.9) | data formatting | bytes 192 | tf_op args[4]
  1.4 0.0 copy-start
  1.4 1.4 %copy-done = bf16[32,3,64,64]{3,2,1,0:T(8,128)(2,1)S(1)} copy-done((bf16[32,3,64,64]{3,2,1,0:T(8,128)(2,1)S(1)}, bf16[32,3,64,64]{3,2,1,0:T(8,128)(2,1)}, u32[]{:S(2)}) %copy-start) | copy-done | bytes 786456
  2.8 0.0 copy-start.1
  2.9 0.9 %copy-done.1 = f32[1,1,8,64,128]{4,3,2,1,0:T(8,128)S(1)} copy-done((f32[1,1,8,64,128]{4,3,2,1,0:T(8,128)S(1)}, f32[1,1,8,64,128]{4,3,2,1,0:T(8,128)}, u32[]{:S(2)}) %copy-start.1) | copy-done | bytes 262168
  3.8 0.0 copy-start.2
  3.8 0.7 %copy-done.2 = s32[3]{0:T(128)S(1)} copy-done((s32[3]{0:T(128)S(1)}, s32[3]{0:T(128)}, u32[]{:S(2)}) %copy-start.2) | copy-done | bytes 36
  4.5 23.7 %shard_map.55 = f32[1,1,8,64,128]{4,3,2,1,0:T(8,128)S(1)} custom-call(f32[1,1,8,64,128]{4,3,2,1,0:T(8,128)S(1)} %copy-done.1, bf16[32,3,64,64]{3,2,1,0:T(8,128)(2,1)S(1)} %copy-done, s32[8,2]{1,0:T(8,128)S(1)} %copy.6.pair_atoms, s32[3]{0:T(128)S(1)} %copy-done.2, f32[2,3,4]{2,1,0:T(4,128)S(1)} %copy.7.weights), custom_call_target="tpu_custom_call" | custom-call | tf_op jit(solution)/shard_map/pallas_call | solution.py:232
  28.2 0.7 %copy.9 = f32[1,1,8,64,128]{4,3,2,1,0:T(8,128)} copy(f32[1,1,8,64,128]{4,3,2,1,0:T(8,128)S(1)} %shard_map.55) | data formatting | bytes 524288
Async XLA Ops:
  1.4 1.4 %copy-start = (bf16[32,3,64,64]{3,2,1,0:T(8,128)(2,1)S(1)}, bf16[32,3,64,64]{3,2,1,0:T(8,128)(2,1)}, u32[]{:S(2)}) copy-start(bf16[32,3,64,64]{3,2,1,0:T(8,128)(2,1)} %couplings_hbm.1) | copy-start | bytes 2359300
  2.8 0.9 %copy-start.1 = (f32[1,1,8,64,128]{4,3,2,1,0:T(8,128)S(1)}, f32[1,1,8,64,128]{4,3,2,1,0:T(8,128)}, u32[]{:S(2)}) copy-start(f32[1,1,8,64,128]{4,3,2,1,0:T(8,128)} %green_hbm.1) | copy-start | bytes 786436
  3.8 0.7 %copy-start.2 = (s32[3]{0:T(128)S(1)}, s32[3]{0:T(128)}, u32[]{:S(2)}) copy-start(s32[3]{0:T(128)} %shift_idx.1) | copy-start | bytes 40

commit v2 on v1

--- a/solution.py
+++ b/solution.py
@@ -27,9 +27,9 @@
 
 def kernel(
     sizes,
-    green_hbm, couplings_hbm, pair_atoms, shift_idx, weights,
+    green_hbm, couplings_hbm, pair_atoms_hbm, shift_idx_hbm, weights_hbm,
     out_ref,
-    green, couplings, packed, held, result, landed, left_table, right_table,
+    green, couplings, pair_atoms, shift_idx, weights, packed, held, result, landed, left_table, right_table,
     load_sem, in_send, in_recv, side_send, side_recv, out_send, out_recv,
 ):
     moms, energies, modes, orbitals, group = sizes
@@ -63,6 +63,13 @@
     load_green.start()
     load_couplings = pltpu.make_async_copy(couplings_hbm, couplings, load_sem.at[1])
     load_couplings.start()
+    load_small = [
+        pltpu.make_async_copy(pair_atoms_hbm, pair_atoms, load_sem.at[2]),
+        pltpu.make_async_copy(shift_idx_hbm, shift_idx, load_sem.at[3]),
+        pltpu.make_async_copy(weights_hbm, weights, load_sem.at[4]),
+    ]
+    for load in load_small:
+        load.start()
 
     edge = jnp.zeros((SHIFT_MAX, rows, lanes), jnp.float32)
     for source in range(moms):
@@ -112,8 +119,10 @@
     held[mom, SHIFT_MAX + here] = packed[half, here]
 
     load_couplings.wait()
-    atom_a = pair_atoms[here, 0]
-    atom_b = pair_atoms[here, 1]
+    for load in load_small:
+        load.wait()
+    atom_a = pair_atoms[0, here]
+    atom_b = pair_atoms[1, here]
     pick_same = (iota((orbitals, lanes), 0) == iota((orbitals, lanes), 1) % orbitals).astype(jnp.bfloat16)
     pick_other = (
         iota((orbitals, lanes), 0) == (iota((orbitals, lanes), 1) + rows) % orbitals
@@ -165,7 +174,7 @@
                     for sign, slot in ((0, energy - shift), (1, energy + shift)):
                         value = held[source, SHIFT_MAX + slot]
                         for target in range(HALVES):
-                            term = weights[sign, mode, (target * cores + offset) % moms] * value
+                            term = weights[mode, sign, (target * cores + offset) % moms] * value
                             totals[target] = term if totals[target] is None else totals[target] + term
                 sums[mode].extend(totals)
         rights = []
@@ -226,24 +235,28 @@
     modes, orbitals = couplings.shape[1], couplings.shape[2]
     lanes, rows, cores = 2 * orbitals, orbitals // 2, moms // HALVES
     group = next(size for size in (4, 2, 1) if energies % size == 0)
-    smem = pl.BlockSpec(memory_space=pltpu.SMEM)
+    atoms_first = pair_atoms.T
+    modes_first = weights.transpose(1, 0, 2)
     hbm = pl.BlockSpec(memory_space=pl.ANY)
     dma = pltpu.SemaphoreType.DMA
     return pl.pallas_call(
         functools.partial(kernel, (moms, energies, modes, orbitals, group)),
         out_shape=jax.ShapeDtypeStruct(green_less.shape, jnp.float32),
-        in_specs=[hbm, hbm, smem, smem, smem],
+        in_specs=[hbm] * 5,
         out_specs=pl.BlockSpec(memory_space=pltpu.VMEM),
         scratch_shapes=[
             pltpu.VMEM(green_less.shape, jnp.float32),
             pltpu.VMEM(couplings.shape, jnp.bfloat16),
+            pltpu.SMEM(atoms_first.shape, jnp.int32),
+            pltpu.SMEM(shift_idx.shape, jnp.int32),
+            pltpu.SMEM(modes_first.shape, jnp.float32),
             pltpu.VMEM((HALVES, energies, rows, lanes), jnp.float32),
             pltpu.VMEM((moms, energies + 2 * SHIFT_MAX, rows, lanes), jnp.float32),
             pltpu.VMEM((HALVES, energies, rows, lanes), jnp.float32),
             pltpu.VMEM((HALVES, energies, rows, lanes), jnp.float32),
             pltpu.VMEM((orbitals, modes * lanes), jnp.bfloat16),
             pltpu.VMEM((modes, lanes, 2 * lanes), jnp.bfloat16),
-            dma((2,)),
+            dma((5,)),
             dma((HALVES, energies)),
             dma((HALVES, energies)),
             dma((cores, HALVES, energies)),
@@ -252,9 +265,9 @@
             dma((HALVES, energies)),
         ],
         compiler_params=pltpu.CompilerParams(
-            collective_id=0, has_side_effects=True, vmem_limit_bytes=40 * 2**20
+            collective_id=0, has_side_effects=True, vmem_limit_bytes=60 * 2**20
         ),
-    )(green_less, couplings, pair_atoms, shift_idx, weights)
+    )(green_less, couplings, atoms_first, shift_idx, modes_first)
 
 
 def solution(mesh):

time: 29.1 us -> 25.5 us (0.88)
  local copies, waits for them, and re-layouts: 5.15 us -> 1.67 us
    unnamed x9 -> x1, local copies, waits for them, and re-layouts: 5.15 us -> 1.67 us
where the time goes in v2:
time: 25.5 us; the launch traced here: 25.4 us
  Pallas kernels  23.7 us (93%)
  local copies, waits for them, and re-layouts  1.67 us (7%)
    pallas_call x1, Pallas kernels, on_device(): pl.pallas_call(functools.partial(kernel, (moms, energies, modes, orbitals...  23.7 us
    unnamed x1, local copies, waits for them, and re-layouts  1.67 us

profile of v2, /device:TPU:11, one launch (start us, length us, event | category | flops | bytes accessed | tf_op | source)
XLA Modules:
  0.0 25.4 jit_solution(16081304750121721399)
XLA Ops:
  0.0 23.7 %shard_map.55 = f32[1,1,8,64,128]{4,3,2,1,0:T(8,128)} custom-call(f32[1,1,8,64,128]{4,3,2,1,0:T(8,128)} %green_hbm.1, bf16[32,3,64,64]{3,2,1,0:T(8,128)(2,1)} %couplings_hbm.1, s32[2,8]{1,0:T(2,128)} %bitcast.3, s32[3]{0:T(128)} %shift_idx_hbm.1, f32[3,2,4]{2,1,0:T(2,128)} %bitcast.2), custom_call_target="tpu_custom_call" | custom-call | tf_op jit(solution)/shard_map/pallas_call | solution.py:242
  23.7 1.7 %copy.7 = f32[1,1,8,64,128]{4,3,2,1,0:T(8,128)} copy(f32[1,1,8,64,128]{4,3,2,1,0:T(8,128)} %shard_map.55) | data formatting | bytes 524288

commit v3 on v2

--- a/solution.py
+++ b/solution.py
@@ -86,35 +86,46 @@
 
     pl.semaphore_wait(barrier, HALVES * energies - 1 + cores - 1)
 
-    def send_in(turn, step):
-        to_half, to = around(half, turn, HALVES), around(here, step, energies)
+    reach = energies // 2
+    place = lax.rem(here, reach)
+
+    def line(far, turn):
+        return lax.rem(here // reach + far, 2) * reach + lax.rem(place + turn, reach)
+
+    def partner(slot):
+        return line(slot // reach, slot % reach)
+
+    def origin(slot):
+        return line(slot // reach, (reach - slot % reach) % reach)
+
+    def send_in(turn, slot):
+        to_half, to = around(half, turn, HALVES), partner(slot)
         return pltpu.make_async_remote_copy(
             src_ref=packed.at[to_half, to],
             dst_ref=held.at[mom, SHIFT_MAX + here],
-            send_sem=in_send.at[turn, step],
-            recv_sem=in_recv.at[turn, step],
+            send_sem=in_send.at[turn, slot],
+            recv_sem=in_recv.at[turn, slot],
             device_id=device(to, to_half, core),
             device_id_type=MESH,
         )
 
-    def send_side(turn, step, side):
+    def send_side(turn, slot, side):
         source = around(half, turn, HALVES) * cores + core
-        slot = SHIFT_MAX + around(here, energies - step, energies)
+        row = SHIFT_MAX + origin(slot)
         return pltpu.make_async_remote_copy(
-            src_ref=held.at[source, slot],
-            dst_ref=held.at[source, slot],
-            send_sem=side_send.at[side, turn, step],
-            recv_sem=side_recv.at[side, turn, step],
+            src_ref=held.at[source, row],
+            dst_ref=held.at[source, row],
+            send_sem=side_send.at[side, turn, slot],
+            recv_sem=side_recv.at[side, turn, slot],
             device_id=device(here, half, around(core, side, cores)),
             device_id_type=MESH,
         )
 
-    far_first = sorted(range(energies), key=lambda step: -min(step, energies - step))
-    slots = [(turn, step) for step in far_first for turn in range(HALVES)]
-    near_first = slots[::-1]
-    remote = [slot for slot in slots if slot != (0, 0)]
-    for turn, step in remote:
-        send_in(turn, step).start()
+    near_first = [(turn, slot) for slot in range(energies) for turn in range(HALVES)]
+    far_first = [(turn, slot) for slot in (*range(reach, energies), *range(reach)) for turn in range(HALVES)]
+    for turn, slot in far_first:
+        if (turn, slot) != (0, 0):
+            send_in(turn, slot).start()
 
     held[mom, SHIFT_MAX + here] = packed[half, here]
 
@@ -140,32 +151,31 @@
         diagonal = jnp.where(same_block, tall.astype(jnp.float32), 0.0).astype(jnp.bfloat16)
         right_table[mode] = jnp.concatenate([diagonal, diagonal], axis=1)
 
-    for turn, step in near_first:
-        if (turn, step) != (0, 0):
-            send_in(turn, step).wait_recv()
+    for turn, slot in near_first:
+        if (turn, slot) != (0, 0):
+            send_in(turn, slot).wait_recv()
         for side in range(1, cores):
-            send_side(turn, step, side).start()
-    for turn, step in near_first:
+            send_side(turn, slot, side).start()
+    for turn, slot in near_first:
         for side in range(1, cores):
-            send_side(turn, step, side).wait_recv()
-
-    def send_out(to_half, to):
-        turn = lax.rem(to_half - half + HALVES, HALVES)
-        step = lax.rem(to - here + energies, energies)
+            send_side(turn, slot, side).wait_recv()
+
+    def send_out(turn, slot):
+        to_half, to = around(half, turn, HALVES), partner(slot)
         return pltpu.make_async_remote_copy(
             src_ref=result.at[to_half, to],
             dst_ref=landed.at[half, here],
-            send_sem=out_send.at[turn, step],
-            recv_sem=out_recv.at[turn, step],
+            send_sem=out_send.at[turn, slot],
+            recv_sem=out_recv.at[turn, slot],
             device_id=device(to, to_half, core),
             device_id_type=MESH,
         )
 
     def one_group(index, carry):
-        first = lax.rem(here // group + 1 + index, energies // group) * group
+        first = lax.rem(reach + index * group, energies)
         sums = [[] for _ in range(modes)]
         for member in range(group):
-            energy = first + member
+            energy = partner(first + member)
             for mode in range(modes):
                 shift = shift_idx[mode]
                 totals = [None] * HALVES
@@ -199,42 +209,43 @@
             product = jnp.dot(
                 left_table[...], jnp.concatenate(columns, axis=1), preferred_element_type=jnp.float32
             )
-            energy = first + member
+            energy = partner(first + member)
             for target in range(HALVES):
                 both = product[:, target * lanes:(target + 1) * lanes]
                 result[target, energy] = jnp.where(mask, both[:rows], both[rows:])
                 own = jnp.logical_and(energy == here, half == target)
+                turn = lax.rem(target - half + HALVES, HALVES)
 
                 @pl.when(jnp.logical_not(own))
                 def _():
-                    send_out(target, energy).start()
+                    send_out(turn, first + member).start()
 
         return carry
 
     lax.fori_loop(0, energies // group, one_group, 0)
     landed[half, here] = result[half, here]
 
-    for step in reversed(far_first):
+    for slot in (*range(reach, energies), *range(reach)):
         for turn in range(HALVES):
-            if (turn, step) != (0, 0):
-                send_out(around(half, turn, HALVES), around(here, step, energies)).wait_recv()
-        pair = around(here, energies - step, energies)
+            if (turn, slot) != (0, 0):
+                send_out(turn, slot).wait_recv()
+        pair = origin(slot)
         real, imag = landed[0, pair], landed[1, pair]
         out_ref[0, 0, pair, pl.ds(0, rows), :] = jnp.where(mask, real, pltpu.roll(imag, orbitals, 1))
         out_ref[0, 0, pair, pl.ds(rows, rows), :] = jnp.where(mask, pltpu.roll(real, orbitals, 1), imag)
 
-    for turn, step in slots:
-        if (turn, step) != (0, 0):
-            send_in(turn, step).wait_send()
-            send_out(around(half, turn, HALVES), around(here, step, energies)).wait_send()
+    for turn, slot in near_first:
+        if (turn, slot) != (0, 0):
+            send_in(turn, slot).wait_send()
+            send_out(turn, slot).wait_send()
         for side in range(1, cores):
-            send_side(turn, step, side).wait_send()
+            send_side(turn, slot, side).wait_send()
 
 
 def on_device(moms, energies, green_less, couplings, pair_atoms, shift_idx, weights):
     modes, orbitals = couplings.shape[1], couplings.shape[2]
     lanes, rows, cores = 2 * orbitals, orbitals // 2, moms // HALVES
-    group = next(size for size in (4, 2, 1) if energies % size == 0)
+    group = next(size for size in (2, 1) if energies // 2 % size == 0)
     atoms_first = pair_atoms.T
     modes_first = weights.transpose(1, 0, 2)
     hbm = pl.BlockSpec(memory_space=pl.ANY)

time: 25.5 us -> 27.9 us (1.094)
  the two profiles are of different devices: /device:TPU:11 before, /device:TPU:0 now
where the time goes in v3:
time: 27.9 us; the launch traced here: 27.8 us
  Pallas kernels  26.1 us (94%)
  local copies, waits for them, and re-layouts  1.67 us (6%)
    pallas_call x1, Pallas kernels, on_device(): pl.pallas_call(functools.partial(kernel, (moms, energies, modes, orbitals...  26.1 us
    unnamed x1, local copies, waits for them, and re-layouts  1.67 us

profile of v3, /device:TPU:0, one launch (start us, length us, event | category | flops | bytes accessed | tf_op | source)
XLA Modules:
  0.0 27.8 jit_solution(12673000304885799114)
XLA Ops:
  0.0 26.1 %shard_map.55 = f32[1,1,8,64,128]{4,3,2,1,0:T(8,128)} custom-call(f32[1,1,8,64,128]{4,3,2,1,0:T(8,128)} %green_hbm.1, bf16[32,3,64,64]{3,2,1,0:T(8,128)(2,1)} %couplings_hbm.1, s32[2,8]{1,0:T(2,128)} %bitcast.3, s32[3]{0:T(128)} %shift_idx_hbm.1, f32[3,2,4]{2,1,0:T(2,128)} %bitcast.2), custom_call_target="tpu_custom_call" | custom-call | tf_op jit(solution)/shard_map/pallas_call | solution.py:253
  26.1 1.7 %copy.7 = f32[1,1,8,64,128]{4,3,2,1,0:T(8,128)} copy(f32[1,1,8,64,128]{4,3,2,1,0:T(8,128)} %shard_map.55) | data formatting | bytes 524288

commit v4 on v2

v4 whole, which is shorter than its diff:
```python
import functools

import jax
import jax.numpy as jnp
from jax import lax
from jax.experimental import pallas as pl
from jax.experimental.pallas import tpu as pltpu
from jax.sharding import PartitionSpec as P

HALVES = 2
ROWS = 2
SHIFT_MAX = 4
MESH = pl.DeviceIdType.MESH


def split(value):
    high = value.astype(jnp.bfloat16)
    return high, (value - high.astype(jnp.float32)).astype(jnp.bfloat16)


def left_lanes(shape):
    return lax.broadcasted_iota(jnp.int32, shape, len(shape) - 1) < shape[-1] // 2


def iota(shape, axis):
    return lax.broadcasted_iota(jnp.int32, shape, axis)


def kernel(
    sizes,
    green_hbm, couplings_hbm, pair_atoms_hbm, shift_idx_hbm, weights_hbm,
    out_hbm,
    green, couplings, pair_atoms, shift_idx, weights, packed, held_real, held_imag, result, landed, out,
    left_table, right_table,
    load_sem, store_sem, in_send, in_recv, up_send, up_recv, side_send, side_recv,
    relay_send, relay_recv, out_send, out_recv,
):
    moms, energies, modes, orbitals, group = sizes
    lanes = 2 * orbitals
    rows = orbitals // 2
    cores = moms // ROWS
    held = (held_real, held_imag)
    here = lax.axis_index("energy")
    mom = lax.axis_index("mom")
    line, core = mom // cores, mom % cores

    def around(base, step, size):
        return lax.rem(base + step, size)

    def along(step):
        return (around(here, step, energies), mom)

    def above(turn):
        return (here, around(line, turn, ROWS) * cores + core)

    def beside(turn):
        return (here, line * cores + around(core, turn, cores))

    barrier = pltpu.get_barrier_semaphore()
    partners = [along(step) for step in range(1, energies)]
    partners += [above(turn) for turn in range(1, ROWS)]
    partners += [beside(turn) for turn in range(1, cores)]
    for partner in partners:
        pl.semaphore_signal(barrier, inc=1, device_id=partner, device_id_type=MESH)

    load_green = pltpu.make_async_copy(green_hbm, green, load_sem.at[0])
    load_green.start()
    load_couplings = pltpu.make_async_copy(couplings_hbm, couplings, load_sem.at[1])
    load_couplings.start()
    load_small = [
        pltpu.make_async_copy(pair_atoms_hbm, pair_atoms, load_sem.at[2]),
        pltpu.make_async_copy(shift_idx_hbm, shift_idx, load_sem.at[3]),
        pltpu.make_async_copy(weights_hbm, weights, load_sem.at[4]),
    ]
    for load in load_small:
        load.start()

    edge = jnp.zeros((SHIFT_MAX, rows, lanes), jnp.float32)
    for half in range(HALVES):
        for source in range(moms):
            held[half][source, pl.ds(0, SHIFT_MAX)] = edge
            held[half][source, pl.ds(SHIFT_MAX + energies, SHIFT_MAX)] = edge

    load_green.wait()
    mask = left_lanes((rows, lanes))
    for pair in range(energies):
        top = green[0, 0, pair, pl.ds(0, rows), :]
        bottom = green[0, 0, pair, pl.ds(rows, rows), :]
        packed[0, pair] = jnp.where(mask, top, pltpu.roll(bottom, orbitals, 1))
        packed[1, pair] = jnp.where(mask, pltpu.roll(top, orbitals, 1), bottom)

    pl.semaphore_wait(barrier, len(partners))

    def remote(source, target, send_sem, recv_sem, device):
        return pltpu.make_async_remote_copy(
            src_ref=source, dst_ref=target, send_sem=send_sem, recv_sem=recv_sem,
            device_id=device, device_id_type=MESH,
        )

    def row(step):
        return SHIFT_MAX + around(here, energies - step, energies)

    def send_in(half, step):
        return remote(
            packed.at[half, around(here, step, energies)], held[half].at[mom, SHIFT_MAX + here],
            in_send.at[half, step], in_recv.at[half, step], along(step),
        )

    def send_up(half, step, turn):
        block = held[half].at[mom, row(step)]
        return remote(block, block, up_send.at[turn, half, step], up_recv.at[turn, half, step], above(turn))

    def send_side(half, step, turn):
        block = held[half].at[mom, row(step)]
        return remote(block, block, side_send.at[turn, half, step], side_recv.at[turn, half, step], beside(turn))

    def send_relay(half, step, up, turn):
        source = around(line, ROWS - up, ROWS) * cores + core
        block = held[half].at[source, row(step)]
        index = (up * cores + turn, half, step)
        return remote(block, block, relay_send.at[index], relay_recv.at[index], beside(turn))

    def send_out(half, step):
        return remote(
            result.at[half, around(here, step, energies)], landed.at[half, here],
            out_send.at[half, step], out_recv.at[half, step], along(step),
        )

    far_first = sorted(range(energies), key=lambda step: -min(step, energies - step))
    near_first = far_first[::-1]
    for half in range(HALVES):
        for step in far_first[:-1]:
            send_in(half, step).start()
    for half in range(HALVES):
        held[half][mom, SHIFT_MAX + here] = packed[half, here]

    load_couplings.wait()
    for load in load_small:
        load.wait()
    atom_a = pair_atoms[0, here]
    atom_b = pair_atoms[1, here]
    pick_same = (iota((orbitals, lanes), 0) == iota((orbitals, lanes), 1) % orbitals).astype(jnp.bfloat16)
    pick_other = (
        iota((orbitals, lanes), 0) == (iota((orbitals, lanes), 1) + rows) % orbitals
    ).astype(jnp.bfloat16)
    upper = iota((orbitals, lanes), 0) < rows
    same_block = (iota((lanes, lanes), 0) < orbitals) == (iota((lanes, lanes), 1) < orbitals)
    for mode in range(modes):
        left = couplings[atom_a, mode]
        right = couplings[atom_b, mode]
        left_same = jnp.dot(left, pick_same, preferred_element_type=jnp.float32)
        left_other = jnp.dot(left, pick_other, preferred_element_type=jnp.float32)
        left_table[:, pl.ds(mode * lanes, lanes)] = jnp.where(upper, left_same, left_other).astype(jnp.bfloat16)
        wide = jnp.dot(right, pick_same, preferred_element_type=jnp.float32).astype(jnp.bfloat16)
        tall = jnp.concatenate([wide, wide], axis=0)
        diagonal = jnp.where(same_block, tall.astype(jnp.float32), 0.0).astype(jnp.bfloat16)
        right_table[mode] = jnp.concatenate([diagonal, diagonal], axis=1)

    def spread(half, steps):
        for step in steps:
            if step:
                send_in(half, step).wait_recv()
            for turn in range(1, ROWS):
                send_up(half, step, turn).start()
            for turn in range(1, cores):
                send_side(half, step, turn).start()

    def pass_on(half):
        for step in near_first:
            for up in range(1, ROWS):
                send_up(half, step, up).wait_recv()
                for turn in range(1, cores):
                    send_relay(half, step, up, turn).start()

    def gather(half):
        for step in near_first:
            for turn in range(1, cores):
                send_side(half, step, turn).wait_recv()
                for up in range(1, ROWS):
                    send_relay(half, step, up, turn).wait_recv()

    def compute(half):
        def one_group(index, carry):
            steps = []
            for member in range(group):
                reach = index * (group // 2) + (member + 1) // 2
                steps.append(energies // 2 + (reach if member % 2 == 0 else -reach))
            sums = [[] for _ in range(modes)]
            for step in steps:
                energy = around(here, step, energies)
                for mode in range(modes):
                    shift = shift_idx[mode]
                    total = None
                    for offset in range(moms):
                        source = lax.rem(mom - offset + moms, moms)
                        for sign, at in ((0, energy - shift), (1, energy + shift)):
                            term = weights[mode, sign, offset] * held[half][source, SHIFT_MAX + at]
                            total = term if total is None else total + term
                    sums[mode].append(total)
            rights = []
            for mode in range(modes):
                high, low = split(jnp.concatenate(sums[mode], axis=0))
                rights.append(
                    lax.dot_general(
                        jnp.concatenate([high, low], axis=1), right_table[mode],
                        (((1,), (1,)), ((), ())), preferred_element_type=jnp.float32,
                    )
                )
            columns = []
            for member in range(group):
                stack = []
                for mode in range(modes):
                    block = rights[mode][member * rows:(member + 1) * rows]
                    high, low = split(jnp.concatenate([block, pltpu.roll(block, orbitals, 1)], axis=0))
                    stack += [high, low]
                columns.append(jnp.concatenate(stack, axis=0))
            product = jnp.dot(
                left_table[...], jnp.concatenate(columns, axis=1), preferred_element_type=jnp.float32
            )
            for member, step in enumerate(steps):
                both = product[:, member * lanes:(member + 1) * lanes]
                result[half, around(here, step, energies)] = jnp.where(mask, both[:rows], both[rows:])

                @pl.when(step > 0)
                def _():
                    send_out(half, step).start()

            return carry

        lax.fori_loop(0, energies // group, one_group, 0)
        landed[half, here] = result[half, here]

    early, late = near_first[:energies // 2], near_first[energies // 2:]
    spread(0, near_first)
    pass_on(0)
    spread(1, early)
    gather(0)
    compute(0)
    spread(1, late)
    pass_on(1)
    gather(1)
    compute(1)

    def store(pair):
        return pltpu.make_async_copy(out.at[0, 0, pair], out_hbm.at[0, 0, pair], store_sem.at[pair])

    for step in (0, *far_first[:-1]):
        if step:
            for half in range(HALVES):
                send_out(half, step).wait_recv()
        pair = around(here, energies - step, energies)
        real, imag = landed[0, pair], landed[1, pair]
        out[0, 0, pair, pl.ds(0, rows), :] = jnp.where(mask, real, pltpu.roll(imag, orbitals, 1))
        out[0, 0, pair, pl.ds(rows, rows), :] = jnp.where(mask, pltpu.roll(real, orbitals, 1), imag)
        store(pair).start()

    for half in range(HALVES):
        for step in near_first:
            if step:
                send_in(half, step).wait_send()
                send_out(half, step).wait_send()
            for turn in range(1, cores):
                send_side(half, step, turn).wait_send()
            for up in range(1, ROWS):
                send_up(half, step, up).wait_send()
                for turn in range(1, cores):
                    send_relay(half, step, up, turn).wait_send()
    for pair in range(energies):
        store(pair).wait()


def on_device(moms, energies, green_less, couplings, pair_atoms, shift_idx, weights):
    modes, orbitals = couplings.shape[1], couplings.shape[2]
    lanes, rows, cores = 2 * orbitals, orbitals // 2, moms // ROWS
    group = next(size for size in (4, 2) if energies % size == 0)
    atoms_first = pair_atoms.T
    modes_first = weights.transpose(1, 0, 2)
    hbm = pl.BlockSpec(memory_space=pl.ANY)
    dma = pltpu.SemaphoreType.DMA
    return pl.pallas_call(
        functools.partial(kernel, (moms, energies, modes, orbitals, group)),
        out_shape=jax.ShapeDtypeStruct(green_less.shape, jnp.float32),
        in_specs=[hbm] * 5,
        out_specs=hbm,
        scratch_shapes=[
            pltpu.VMEM(green_less.shape, jnp.float32),
            pltpu.VMEM(couplings.shape, jnp.bfloat16),
            pltpu.SMEM(atoms_first.shape, jnp.int32),
            pltpu.SMEM(shift_idx.shape, jnp.int32),
            pltpu.SMEM(modes_first.shape, jnp.float32),
            pltpu.VMEM((HALVES, energies, rows, lanes), jnp.float32),
            pltpu.VMEM((moms, energies + 2 * SHIFT_MAX, rows, lanes), jnp.float32),
            pltpu.VMEM((moms, energies + 2 * SHIFT_MAX, rows, lanes), jnp.float32),
            pltpu.VMEM((HALVES, energies, rows, lanes), jnp.float32),
            pltpu.VMEM((HALVES, energies, rows, lanes), jnp.float32),
            pltpu.VMEM(green_less.shape, jnp.float32),
            pltpu.VMEM((orbitals, modes * lanes), jnp.bfloat16),
            pltpu.VMEM((modes, lanes, 2 * lanes), jnp.bfloat16),
            dma((5,)),
            dma((energies,)),
            dma((HALVES, energies)),
            dma((HALVES, energies)),
            dma((ROWS, HALVES, energies)),
            dma((ROWS, HALVES, energies)),
            dma((cores, HALVES, energies)),
            dma((cores, HALVES, energies)),
            dma((ROWS * cores, HALVES, energies)),
            dma((ROWS * cores, HALVES, energies)),
            dma((HALVES, energies)),
            dma((HALVES, energies)),
        ],
        compiler_params=pltpu.CompilerParams(
            collective_id=0, has_side_effects=True, vmem_limit_bytes=60 * 2**20
        ),
    )(green_less, couplings, atoms_first, shift_idx, modes_first)


def solution(mesh):
    spec = P("mom", "energy", None, None, None)
    return jax.shard_map(
        functools.partial(on_device, mesh.shape["mom"], mesh.shape["energy"]),
        mesh=mesh,
        in_specs=(spec, P(), P(), P(), P()),
        out_specs=spec,
        check_vma=False,
    )
```

time: 25.5 us -> 33.4 us (1.31)
  the two profiles are of different devices: /device:TPU:11 before, /device:TPU:0 now
where the time goes in v4:
time: 33.4 us; the launch traced here: 33.3 us
  Pallas kernels  31.6 us (95%)
  local copies, waits for them, and re-layouts  1.67 us (5%)
    pallas_call x1, Pallas kernels, on_device(): pl.pallas_call(functools.partial(kernel, (moms, energies, modes, orbitals...  31.6 us
    unnamed x1, local copies, waits for them, and re-layouts  1.67 us

profile of v4, /device:TPU:0, one launch (start us, length us, event | category | flops | bytes accessed | tf_op | source)
XLA Modules:
  0.0 33.3 jit_solution(14673485694037419021)
XLA Ops:
  0.0 31.6 %shard_map.55 = f32[1,1,8,64,128]{4,3,2,1,0:T(8,128)} custom-call(f32[1,1,8,64,128]{4,3,2,1,0:T(8,128)} %green_hbm.1, bf16[32,3,64,64]{3,2,1,0:T(8,128)(2,1)} %couplings_hbm.1, s32[2,8]{1,0:T(2,128)} %bitcast.3, s32[3]{0:T(128)} %shift_idx_hbm.1, f32[3,2,4]{2,1,0:T(2,128)} %bitcast.2), custom_call_target="tpu_custom_call" | custom-call | tf_op jit(solution)/shard_map/pallas_call | solution.py:280
  31.6 1.7 %copy.7 = f32[1,1,8,64,128]{4,3,2,1,0:T(8,128)} copy(f32[1,1,8,64,128]{4,3,2,1,0:T(8,128)} %shard_map.55) | data formatting | bytes 524288

commit v5 on v2

--- a/solution.py
+++ b/solution.py
@@ -28,11 +28,12 @@
 def kernel(
     sizes,
     green_hbm, couplings_hbm, pair_atoms_hbm, shift_idx_hbm, weights_hbm,
-    out_ref,
-    green, couplings, pair_atoms, shift_idx, weights, packed, held, result, landed, left_table, right_table,
-    load_sem, in_send, in_recv, side_send, side_recv, out_send, out_recv,
+    out_hbm,
+    green, couplings, pair_atoms, shift_idx, weights, packed, held, result, landed, out, left_table, right_table,
+    load_sem, store_sem, in_send, in_recv, side_send, side_recv, out_send, out_recv,
 ):
     moms, energies, modes, orbitals, group = sizes
+    reach = energies // 2
     lanes = 2 * orbitals
     rows = orbitals // 2
     cores = moms // HALVES
@@ -92,22 +93,36 @@
             src_ref=packed.at[to_half, to],
             dst_ref=held.at[mom, SHIFT_MAX + here],
             send_sem=in_send.at[turn, step],
-            recv_sem=in_recv.at[turn, step],
+            recv_sem=in_recv.at[turn, here],
             device_id=device(to, to_half, core),
             device_id_type=MESH,
         )
 
-    def send_side(turn, step, side):
+    def send_side(turn, far, side):
         source = around(half, turn, HALVES) * cores + core
-        slot = SHIFT_MAX + around(here, energies - step, energies)
+        base = around(here // reach, far, energies // reach) * reach
+        block = held.at[source, pl.ds(SHIFT_MAX + base, reach)]
         return pltpu.make_async_remote_copy(
-            src_ref=held.at[source, slot],
-            dst_ref=held.at[source, slot],
-            send_sem=side_send.at[side, turn, step],
-            recv_sem=side_recv.at[side, turn, step],
+            src_ref=block,
+            dst_ref=block,
+            send_sem=side_send.at[side, turn, far],
+            recv_sem=side_recv.at[side, turn, far],
             device_id=device(here, half, around(core, side, cores)),
             device_id_type=MESH,
         )
+
+    def arrive_in(turn, source):
+        def wait():
+            slot = held.at[around(half, turn, HALVES) * cores + core, SHIFT_MAX + source]
+            pltpu.make_async_remote_copy(
+                src_ref=slot, dst_ref=slot, send_sem=in_send.at[turn, 0], recv_sem=in_recv.at[turn, source],
+                device_id=device(here, half, around(core, 1, cores)), device_id_type=MESH,
+            ).wait_recv()
+
+        if turn == 0:
+            pl.when(source != here)(wait)
+        else:
+            wait()
 
     far_first = sorted(range(energies), key=lambda step: -min(step, energies - step))
     slots = [(turn, step) for step in far_first for turn in range(HALVES)]
@@ -135,19 +150,23 @@
         left_same = jnp.dot(left, pick_same, preferred_element_type=jnp.float32)
         left_other = jnp.dot(left, pick_other, preferred_element_type=jnp.float32)
         left_table[:, pl.ds(mode * lanes, lanes)] = jnp.where(upper, left_same, left_other).astype(jnp.bfloat16)
-        wide = jnp.dot(right, pick_same, preferred_element_type=jnp.float32).astype(jnp.bfloat16)
+        wide = lax.dot_general(
+            right, pick_same, (((0,), (0,)), ((), ())), preferred_element_type=jnp.float32
+        ).astype(jnp.bfloat16)
         tall = jnp.concatenate([wide, wide], axis=0)
         diagonal = jnp.where(same_block, tall.astype(jnp.float32), 0.0).astype(jnp.bfloat16)
-        right_table[mode] = jnp.concatenate([diagonal, diagonal], axis=1)
-
-    for turn, step in near_first:
-        if (turn, step) != (0, 0):
-            send_in(turn, step).wait_recv()
+        right_table[mode] = jnp.concatenate([diagonal, diagonal], axis=0)
+
+    chunks = [(turn, far) for far in range(energies // reach) for turn in range(HALVES)]
+    for turn, far in chunks:
+        base = around(here // reach, far, energies // reach) * reach
+        for member in range(reach):
+            arrive_in(turn, base + member)
         for side in range(1, cores):
-            send_side(turn, step, side).start()
-    for turn, step in near_first:
+            send_side(turn, far, side).start()
+    for turn, far in chunks:
         for side in range(1, cores):
-            send_side(turn, step, side).wait_recv()
+            send_side(turn, far, side).wait_recv()
 
     def send_out(to_half, to):
         turn = lax.rem(to_half - half + HALVES, HALVES)
@@ -181,9 +200,9 @@
         for mode in range(modes):
             high, low = split(jnp.concatenate(sums[mode], axis=0))
             rights.append(
-                lax.dot_general(
+                jnp.dot(
                     jnp.concatenate([high, low], axis=1), right_table[mode],
-                    (((1,), (1,)), ((), ())), preferred_element_type=jnp.float32,
+                    preferred_element_type=jnp.float32,
                 )
             )
         for member in range(group):
@@ -214,21 +233,28 @@
     lax.fori_loop(0, energies // group, one_group, 0)
     landed[half, here] = result[half, here]
 
+    def store(pair):
+        return pltpu.make_async_copy(out.at[0, 0, pair], out_hbm.at[0, 0, pair], store_sem.at[pair])
+
     for step in reversed(far_first):
         for turn in range(HALVES):
             if (turn, step) != (0, 0):
                 send_out(around(half, turn, HALVES), around(here, step, energies)).wait_recv()
         pair = around(here, energies - step, energies)
         real, imag = landed[0, pair], landed[1, pair]
-        out_ref[0, 0, pair, pl.ds(0, rows), :] = jnp.where(mask, real, pltpu.roll(imag, orbitals, 1))
-        out_ref[0, 0, pair, pl.ds(rows, rows), :] = jnp.where(mask, pltpu.roll(real, orbitals, 1), imag)
+        out[0, 0, pair, pl.ds(0, rows), :] = jnp.where(mask, real, pltpu.roll(imag, orbitals, 1))
+        out[0, 0, pair, pl.ds(rows, rows), :] = jnp.where(mask, pltpu.roll(real, orbitals, 1), imag)
+        store(pair).start()
 
     for turn, step in slots:
         if (turn, step) != (0, 0):
             send_in(turn, step).wait_send()
             send_out(around(half, turn, HALVES), around(here, step, energies)).wait_send()
+    for turn, far in chunks:
         for side in range(1, cores):
-            send_side(turn, step, side).wait_send()
+            send_side(turn, far, side).wait_send()
+    for pair in range(energies):
+        store(pair).wait()
 
 
 def on_device(moms, energies, green_less, couplings, pair_atoms, shift_idx, weights):
@@ -243,7 +269,7 @@
         functools.partial(kernel, (moms, energies, modes, orbitals, group)),
         out_shape=jax.ShapeDtypeStruct(green_less.shape, jnp.float32),
         in_specs=[hbm] * 5,
-        out_specs=pl.BlockSpec(memory_space=pltpu.VMEM),
+        out_specs=hbm,
         scratch_shapes=[
             pltpu.VMEM(green_less.shape, jnp.float32),
             pltpu.VMEM(couplings.shape, jnp.bfloat16),
@@ -254,13 +280,15 @@
             pltpu.VMEM((moms, energies + 2 * SHIFT_MAX, rows, lanes), jnp.float32),
             pltpu.VMEM((HALVES, energies, rows, lanes), jnp.float32),
             pltpu.VMEM((HALVES, energies, rows, lanes), jnp.float32),
+            pltpu.VMEM(green_less.shape, jnp.float32),
             pltpu.VMEM((orbitals, modes * lanes), jnp.bfloat16),
-            pltpu.VMEM((modes, lanes, 2 * lanes), jnp.bfloat16),
+            pltpu.VMEM((modes, 2 * lanes, lanes), jnp.bfloat16),
             dma((5,)),
+            dma((energies,)),
             dma((HALVES, energies)),
             dma((HALVES, energies)),
-            dma((cores, HALVES, energies)),
-            dma((cores, HALVES, energies)),
+            dma((cores, HALVES, 2)),
+            dma((cores, HALVES, 2)),
             dma((HALVES, energies)),
             dma((HALVES, energies)),
         ],

time: 25.5 us -> 24.9 us (0.976)
  the two profiles are of different devices: /device:TPU:11 before, /device:TPU:0 now
where the time goes in v5:
time: 24.9 us; the launch traced here: 24.6 us
  Pallas kernels  22.9 us (92%)
  local copies, waits for them, and re-layouts  1.67 us (7%)
    pallas_call x1, Pallas kernels, on_device(): pl.pallas_call(functools.partial(kernel, (moms, energies, modes, orbitals...  22.9 us
    unnamed x1, local copies, waits for them, and re-layouts  1.67 us

profile of v5, /device:TPU:0, one launch (start us, length us, event | category | flops | bytes accessed | tf_op | source)
XLA Modules:
  0.0 24.6 jit_solution(10530629801679408824)
XLA Ops:
  0.0 22.9 %shard_map.55 = f32[1,1,8,64,128]{4,3,2,1,0:T(8,128)} custom-call(f32[1,1,8,64,128]{4,3,2,1,0:T(8,128)} %green_hbm.1, bf16[32,3,64,64]{3,2,1,0:T(8,128)(2,1)} %couplings_hbm.1, s32[2,8]{1,0:T(2,128)} %bitcast.3, s32[3]{0:T(128)} %shift_idx_hbm.1, f32[3,2,4]{2,1,0:T(2,128)} %bitcast.2), custom_call_target="tpu_custom_call" | custom-call | tf_op jit(solution)/shard_map/pallas_call | solution.py:268
  22.9 1.7 %copy.7 = f32[1,1,8,64,128]{4,3,2,1,0:T(8,128)} copy(f32[1,1,8,64,128]{4,3,2,1,0:T(8,128)} %shard_map.55) | data formatting | bytes 524288

commit v6 on v5

--- a/solution.py
+++ b/solution.py
@@ -28,9 +28,9 @@
 def kernel(
     sizes,
     green_hbm, couplings_hbm, pair_atoms_hbm, shift_idx_hbm, weights_hbm,
-    out_hbm,
-    green, couplings, pair_atoms, shift_idx, weights, packed, held, result, landed, out, left_table, right_table,
-    load_sem, store_sem, in_send, in_recv, side_send, side_recv, out_send, out_recv,
+    out,
+    green, couplings, pair_atoms, shift_idx, weights, packed, held, aside, partial, result, landed, left_table, right_table,
+    load_sem, in_send, in_recv, side_send, side_recv, out_send, out_recv,
 ):
     moms, energies, modes, orbitals, group = sizes
     reach = energies // 2
@@ -73,9 +73,12 @@
         load.start()
 
     edge = jnp.zeros((SHIFT_MAX, rows, lanes), jnp.float32)
-    for source in range(moms):
+    for source in range(HALVES):
         held[source, pl.ds(0, SHIFT_MAX)] = edge
         held[source, pl.ds(SHIFT_MAX + energies, SHIFT_MAX)] = edge
+        for side in range(1, cores):
+            aside[side - 1, source, pl.ds(0, SHIFT_MAX)] = edge
+            aside[side - 1, source, pl.ds(SHIFT_MAX + energies, SHIFT_MAX)] = edge
 
     load_green.wait()
     mask = left_lanes((rows, lanes))
@@ -91,7 +94,7 @@
         to_half, to = around(half, turn, HALVES), around(here, step, energies)
         return pltpu.make_async_remote_copy(
             src_ref=packed.at[to_half, to],
-            dst_ref=held.at[mom, SHIFT_MAX + here],
+            dst_ref=held.at[half, SHIFT_MAX + here],
             send_sem=in_send.at[turn, step],
             recv_sem=in_recv.at[turn, here],
             device_id=device(to, to_half, core),
@@ -99,12 +102,12 @@
         )
 
     def send_side(turn, far, side):
-        source = around(half, turn, HALVES) * cores + core
+        source = around(half, turn, HALVES)
         base = around(here // reach, far, energies // reach) * reach
-        block = held.at[source, pl.ds(SHIFT_MAX + base, reach)]
+        block = pl.ds(SHIFT_MAX + base, reach)
         return pltpu.make_async_remote_copy(
-            src_ref=block,
-            dst_ref=block,
+            src_ref=held.at[source, block],
+            dst_ref=aside.at[side - 1, source, block],
             send_sem=side_send.at[side, turn, far],
             recv_sem=side_recv.at[side, turn, far],
             device_id=device(here, half, around(core, side, cores)),
@@ -113,7 +116,7 @@
 
     def arrive_in(turn, source):
         def wait():
-            slot = held.at[around(half, turn, HALVES) * cores + core, SHIFT_MAX + source]
+            slot = held.at[around(half, turn, HALVES), SHIFT_MAX + source]
             pltpu.make_async_remote_copy(
                 src_ref=slot, dst_ref=slot, send_sem=in_send.at[turn, 0], recv_sem=in_recv.at[turn, source],
                 device_id=device(here, half, around(core, 1, cores)), device_id_type=MESH,
@@ -131,7 +134,7 @@
     for turn, step in remote:
         send_in(turn, step).start()
 
-    held[mom, SHIFT_MAX + here] = packed[half, here]
+    held[half, SHIFT_MAX + here] = packed[half, here]
 
     load_couplings.wait()
     for load in load_small:
@@ -164,6 +167,29 @@
             arrive_in(turn, base + member)
         for side in range(1, cores):
             send_side(turn, far, side).start()
+    def mix(block, energy, mode, offset, totals):
+        shift = shift_idx[mode]
+        for row in range(HALVES):
+            source = lax.rem(row + HALVES - (offset > core).astype(jnp.int32), HALVES)
+            for sign, slot in ((0, energy - shift), (1, energy + shift)):
+                value = block[source, SHIFT_MAX + slot]
+                for target in range(HALVES):
+                    turn = ((target - row) * cores + offset) % moms
+                    term = weights[mode, sign, turn] * value
+                    totals[target] = term if totals[target] is None else totals[target] + term
+        return totals
+
+    def own_part(index, carry):
+        for member in range(group):
+            energy = index * group + member
+            for mode in range(modes):
+                totals = mix(held, energy, mode, 0, [None] * HALVES)
+                for target in range(HALVES):
+                    partial[mode, energy, target] = totals[target]
+        return carry
+
+    lax.fori_loop(0, energies // group, own_part, 0)
+
     for turn, far in chunks:
         for side in range(1, cores):
             send_side(turn, far, side).wait_recv()
@@ -180,21 +206,17 @@
             device_id_type=MESH,
         )
 
+    order = sorted(range(group), key=lambda member: min(member, 1 + group - 1 - member))
+
     def one_group(index, carry):
         first = lax.rem(here // group + 1 + index, energies // group) * group
         sums = [[] for _ in range(modes)]
         for member in range(group):
-            energy = first + member
+            energy = first + order[member]
             for mode in range(modes):
-                shift = shift_idx[mode]
-                totals = [None] * HALVES
-                for offset in range(moms):
-                    source = lax.rem(core - offset + moms, moms)
-                    for sign, slot in ((0, energy - shift), (1, energy + shift)):
-                        value = held[source, SHIFT_MAX + slot]
-                        for target in range(HALVES):
-                            term = weights[mode, sign, (target * cores + offset) % moms] * value
-                            totals[target] = term if totals[target] is None else totals[target] + term
+                totals = [partial[mode, energy, target] for target in range(HALVES)]
+                for side in range(1, cores):
+                    totals = mix(aside.at[side - 1], energy, mode, side, totals)
                 sums[mode].extend(totals)
         rights = []
         for mode in range(modes):
@@ -218,7 +240,7 @@
             product = jnp.dot(
                 left_table[...], jnp.concatenate(columns, axis=1), preferred_element_type=jnp.float32
             )
-            energy = first + member
+            energy = first + order[member]
             for target in range(HALVES):
                 both = product[:, target * lanes:(target + 1) * lanes]
                 result[target, energy] = jnp.where(mask, both[:rows], both[rows:])
@@ -232,9 +254,6 @@
 
     lax.fori_loop(0, energies // group, one_group, 0)
     landed[half, here] = result[half, here]
-
-    def store(pair):
-        return pltpu.make_async_copy(out.at[0, 0, pair], out_hbm.at[0, 0, pair], store_sem.at[pair])
 
     for step in reversed(far_first):
         for turn in range(HALVES):
@@ -244,7 +263,6 @@
         real, imag = landed[0, pair], landed[1, pair]
         out[0, 0, pair, pl.ds(0, rows), :] = jnp.where(mask, real, pltpu.roll(imag, orbitals, 1))
         out[0, 0, pair, pl.ds(rows, rows), :] = jnp.where(mask, pltpu.roll(real, orbitals, 1), imag)
-        store(pair).start()
 
     for turn, step in slots:
         if (turn, step) != (0, 0):
@@ -253,8 +271,6 @@
     for turn, far in chunks:
         for side in range(1, cores):
             send_side(turn, far, side).wait_send()
-    for pair in range(energies):
-        store(pair).wait()
 
 
 def on_device(moms, energies, green_less, couplings, pair_atoms, shift_idx, weights):
@@ -267,9 +283,9 @@
     dma = pltpu.SemaphoreType.DMA
     return pl.pallas_call(
         functools.partial(kernel, (moms, energies, modes, orbitals, group)),
-        out_shape=jax.ShapeDtypeStruct(green_less.shape, jnp.float32),
+        out_shape=pltpu.VMEM(green_less.shape, jnp.float32),
         in_specs=[hbm] * 5,
-        out_specs=hbm,
+        out_specs=pl.BlockSpec(memory_space=pltpu.VMEM),
         scratch_shapes=[
             pltpu.VMEM(green_less.shape, jnp.float32),
             pltpu.VMEM(couplings.shape, jnp.bfloat16),
@@ -277,14 +293,14 @@
             pltpu.SMEM(shift_idx.shape, jnp.int32),
             pltpu.SMEM(modes_first.shape, jnp.float32),
             pltpu.VMEM((HALVES, energies, rows, lanes), jnp.float32),
-            pltpu.VMEM((moms, energies + 2 * SHIFT_MAX, rows, lanes), jnp.float32),
+            pltpu.VMEM((HALVES, energies + 2 * SHIFT_MAX, rows, lanes), jnp.float32),
+            pltpu.VMEM((cores - 1, HALVES, energies + 2 * SHIFT_MAX, rows, lanes), jnp.float32),
+            pltpu.VMEM((modes, energies, HALVES, rows, lanes), jnp.float32),
             pltpu.VMEM((HALVES, energies, rows, lanes), jnp.float32),
             pltpu.VMEM((HALVES, energies, rows, lanes), jnp.float32),
-            pltpu.VMEM(green_less.shape, jnp.float32),
             pltpu.VMEM((orbitals, modes * lanes), jnp.bfloat16),
             pltpu.VMEM((modes, 2 * lanes, lanes), jnp.bfloat16),
             dma((5,)),
-            dma((energies,)),
             dma((HALVES, energies)),
             dma((HALVES, energies)),
             dma((cores, HALVES, 2)),
@@ -293,7 +309,7 @@
             dma((HALVES, energies)),
         ],
         compiler_params=pltpu.CompilerParams(
-            collective_id=0, has_side_effects=True, vmem_limit_bytes=60 * 2**20
+            collective_id=0, has_side_effects=True, vmem_limit_bytes=58 * 2**20
         ),
     )(green_less, couplings, atoms_first, shift_idx, modes_first)
 

time: 24.9 us -> 23.3 us (0.936)
  local copies, waits for them, and re-layouts: 1.67 us -> 0.71 us
  Pallas kernels: 22.9 us -> 22.4 us
    unnamed x1, local copies, waits for them, and re-layouts: 1.67 us -> 0.71 us
    pallas_call x1, Pallas kernels: 22.9 us -> 22.4 us  [on_device(): pl.pallas_call(functools.partial(kernel, (moms, energies, modes, orbitals...]
where the time goes in v6:
time: 23.3 us; the launch traced here: 23.1 us
  Pallas kernels  22.4 us (96%)
  local copies, waits for them, and re-layouts  0.71 us (3%)
    pallas_call x1, Pallas kernels, on_device(): pl.pallas_call(functools.partial(kernel, (moms, energies, modes, orbitals...  22.4 us
    unnamed x1, local copies, waits for them, and re-layouts  0.71 us

profile of v6, /device:TPU:0, one launch (start us, length us, event | category | flops | bytes accessed | tf_op | source)
XLA Modules:
  0.0 23.1 jit_solution(1015364536078845895)
XLA Ops:
  0.0 22.4 %shard_map.55 = f32[1,1,8,64,128]{4,3,2,1,0:T(8,128)S(1)} custom-call(f32[1,1,8,64,128]{4,3,2,1,0:T(8,128)} %green_hbm.1, bf16[32,3,64,64]{3,2,1,0:T(8,128)(2,1)} %couplings_hbm.1, s32[2,8]{1,0:T(2,128)} %bitcast.3, s32[3]{0:T(128)} %shift_idx_hbm.1, f32[3,2,4]{2,1,0:T(2,128)} %bitcast.2), custom_call_target="tpu_custom_call" | custom-call | tf_op jit(solution)/shard_map/pallas_call | solution.py:284
  22.4 0.7 %copy.7 = f32[1,1,8,64,128]{4,3,2,1,0:T(8,128)} copy(f32[1,1,8,64,128]{4,3,2,1,0:T(8,128)S(1)} %shard_map.55) | data formatting | bytes 524288

commit v7 on v6

--- a/solution.py
+++ b/solution.py
@@ -206,13 +206,14 @@
             device_id_type=MESH,
         )
 
-    order = sorted(range(group), key=lambda member: min(member, 1 + group - 1 - member))
+    place = lax.rem(here, reach)
 
     def one_group(index, carry):
-        first = lax.rem(here // group + 1 + index, energies // group) * group
+        chosen = [
+            around(here // reach, 1 - side, 2) * reach + lax.rem(place + index + side, reach) for side in range(group)
+        ]
         sums = [[] for _ in range(modes)]
-        for member in range(group):
-            energy = first + order[member]
+        for energy in chosen:
             for mode in range(modes):
                 totals = [partial[mode, energy, target] for target in range(HALVES)]
                 for side in range(1, cores):
@@ -240,7 +241,7 @@
             product = jnp.dot(
                 left_table[...], jnp.concatenate(columns, axis=1), preferred_element_type=jnp.float32
             )
-            energy = first + order[member]
+            energy = chosen[member]
             for target in range(HALVES):
                 both = product[:, target * lanes:(target + 1) * lanes]
                 result[target, energy] = jnp.where(mask, both[:rows], both[rows:])
@@ -276,7 +277,7 @@
 def on_device(moms, energies, green_less, couplings, pair_atoms, shift_idx, weights):
     modes, orbitals = couplings.shape[1], couplings.shape[2]
     lanes, rows, cores = 2 * orbitals, orbitals // 2, moms // HALVES
-    group = next(size for size in (4, 2, 1) if energies % size == 0)
+    group = 2
     atoms_first = pair_atoms.T
     modes_first = weights.transpose(1, 0, 2)
     hbm = pl.BlockSpec(memory_space=pl.ANY)

time: 23.3 us -> 23.4 us (level)
  no operation moved by 1% of the time
where the time goes in v7:
time: 23.4 us; the launch traced here: 23 us
  Pallas kernels  22.3 us (95%)
  local copies, waits for them, and re-layouts  0.71 us (3%)
    pallas_call x1, Pallas kernels, on_device(): pl.pallas_call(functools.partial(kernel, (moms, energies, modes, orbitals...  22.3 us
    unnamed x1, local copies, waits for them, and re-layouts  0.71 us

profile of v7, /device:TPU:0, one launch (start us, length us, event | category | flops | bytes accessed | tf_op | source)
XLA Modules:
  0.0 23.0 jit_solution(8284758600200506445)
XLA Ops:
  0.0 22.3 %shard_map.55 = f32[1,1,8,64,128]{4,3,2,1,0:T(8,128)S(1)} custom-call(f32[1,1,8,64,128]{4,3,2,1,0:T(8,128)} %green_hbm.1, bf16[32,3,64,64]{3,2,1,0:T(8,128)(2,1)} %couplings_hbm.1, s32[2,8]{1,0:T(2,128)} %bitcast.3, s32[3]{0:T(128)} %shift_idx_hbm.1, f32[3,2,4]{2,1,0:T(2,128)} %bitcast.2), custom_call_target="tpu_custom_call" | custom-call | tf_op jit(solution)/shard_map/pallas_call | solution.py:285
  22.3 0.7 %copy.7 = f32[1,1,8,64,128]{4,3,2,1,0:T(8,128)} copy(f32[1,1,8,64,128]{4,3,2,1,0:T(8,128)S(1)} %shard_map.55) | data formatting | bytes 524288

commit v8 on v7

--- a/solution.py
+++ b/solution.py
@@ -62,6 +62,15 @@
 
     load_green = pltpu.make_async_copy(green_hbm, green, load_sem.at[0])
     load_green.start()
+    edge = jnp.zeros((SHIFT_MAX, rows, lanes), jnp.float32)
+    for source in range(HALVES):
+        held[source, pl.ds(0, SHIFT_MAX)] = edge
+        held[source, pl.ds(SHIFT_MAX + energies, SHIFT_MAX)] = edge
+        for side in range(1, cores):
+            aside[side - 1, source, pl.ds(0, SHIFT_MAX)] = edge
+            aside[side - 1, source, pl.ds(SHIFT_MAX + energies, SHIFT_MAX)] = edge
+
+    load_green.wait()
     load_couplings = pltpu.make_async_copy(couplings_hbm, couplings, load_sem.at[1])
     load_couplings.start()
     load_small = [
@@ -71,16 +80,6 @@
     ]
     for load in load_small:
         load.start()
-
-    edge = jnp.zeros((SHIFT_MAX, rows, lanes), jnp.float32)
-    for source in range(HALVES):
-        held[source, pl.ds(0, SHIFT_MAX)] = edge
-        held[source, pl.ds(SHIFT_MAX + energies, SHIFT_MAX)] = edge
-        for side in range(1, cores):
-            aside[side - 1, source, pl.ds(0, SHIFT_MAX)] = edge
-            aside[side - 1, source, pl.ds(SHIFT_MAX + energies, SHIFT_MAX)] = edge
-
-    load_green.wait()
     mask = left_lanes((rows, lanes))
     for pair in range(energies):
         top = green[0, 0, pair, pl.ds(0, rows), :]
@@ -101,15 +100,19 @@
             device_id_type=MESH,
         )
 
-    def send_side(turn, far, side):
+    piece = reach // 2
+
+    def base_of(part):
+        return around(here // reach, part // 2, 2) * reach + part % 2 * piece
+
+    def send_side(turn, part, side):
         source = around(half, turn, HALVES)
-        base = around(here // reach, far, energies // reach) * reach
-        block = pl.ds(SHIFT_MAX + base, reach)
+        block = pl.ds(SHIFT_MAX + base_of(part), piece)
         return pltpu.make_async_remote_copy(
             src_ref=held.at[source, block],
             dst_ref=aside.at[side - 1, source, block],
-            send_sem=side_send.at[side, turn, far],
-            recv_sem=side_recv.at[side, turn, far],
+            send_sem=side_send.at[side, turn, part],
+            recv_sem=side_recv.at[side, turn, part],
             device_id=device(here, half, around(core, side, cores)),
             device_id_type=MESH,
         )
@@ -130,9 +133,13 @@
     far_first = sorted(range(energies), key=lambda step: -min(step, energies - step))
     slots = [(turn, step) for step in far_first for turn in range(HALVES)]
     near_first = slots[::-1]
-    remote = [slot for slot in slots if slot != (0, 0)]
-    for turn, step in remote:
-        send_in(turn, step).start()
+    place = lax.rem(here, reach)
+    for index in range(reach):
+        for side in range(2):
+            to = around(here // reach, 1 - side, 2) * reach + lax.rem(place + index + side, reach)
+            for turn in range(HALVES):
+                if (turn, side, index) != (0, 1, reach - 1):
+                    send_in(turn, lax.rem(to - here + energies, energies)).start()
 
     held[half, SHIFT_MAX + here] = packed[half, here]
 
@@ -160,13 +167,12 @@
         diagonal = jnp.where(same_block, tall.astype(jnp.float32), 0.0).astype(jnp.bfloat16)
         right_table[mode] = jnp.concatenate([diagonal, diagonal], axis=0)
 
-    chunks = [(turn, far) for far in range(energies // reach) for turn in range(HALVES)]
-    for turn, far in chunks:
-        base = around(here // reach, far, energies // reach) * reach
-        for member in range(reach):
-            arrive_in(turn, base + member)
+    chunks = [(turn, part) for part in range(energies // piece) for turn in range(HALVES)]
+    for turn, part in chunks:
+        for member in range(piece):
+            arrive_in(turn, base_of(part) + member)
         for side in range(1, cores):
-            send_side(turn, far, side).start()
+            send_side(turn, part, side).start()
     def mix(block, energy, mode, offset, totals):
         shift = shift_idx[mode]
         for row in range(HALVES):
@@ -190,9 +196,9 @@
 
     lax.fori_loop(0, energies // group, own_part, 0)
 
-    for turn, far in chunks:
+    for turn, part in chunks:
         for side in range(1, cores):
-            send_side(turn, far, side).wait_recv()
+            send_side(turn, part, side).wait_recv()
 
     def send_out(to_half, to):
         turn = lax.rem(to_half - half + HALVES, HALVES)
@@ -205,8 +211,6 @@
             device_id=device(to, to_half, core),
             device_id_type=MESH,
         )
-
-    place = lax.rem(here, reach)
 
     def one_group(index, carry):
         chosen = [
@@ -269,9 +273,9 @@
         if (turn, step) != (0, 0):
             send_in(turn, step).wait_send()
             send_out(around(half, turn, HALVES), around(here, step, energies)).wait_send()
-    for turn, far in chunks:
+    for turn, part in chunks:
         for side in range(1, cores):
-            send_side(turn, far, side).wait_send()
+            send_side(turn, part, side).wait_send()
 
 
 def on_device(moms, energies, green_less, couplings, pair_atoms, shift_idx, weights):
@@ -304,8 +308,8 @@
             dma((5,)),
             dma((HALVES, energies)),
             dma((HALVES, energies)),
-            dma((cores, HALVES, 2)),
-            dma((cores, HALVES, 2)),
+            dma((cores, HALVES, 4)),
+            dma((cores, HALVES, 4)),
             dma((HALVES, energies)),
             dma((HALVES, energies)),
         ],

time: 23.4 us -> 26 us (1.11); the launches traced: 23 us -> 25.9 us
  Pallas kernels: 22.3 us -> 25.2 us
    pallas_call x1, Pallas kernels: 22.3 us -> 25.2 us  [on_device(): pl.pallas_call(functools.partial(kernel, (moms, energies, modes, orbitals...]
where the time goes in v8:
time: 26 us; the launch traced here: 25.9 us
  Pallas kernels  25.2 us (97%)
  local copies, waits for them, and re-layouts  0.71 us (3%)
    pallas_call x1, Pallas kernels, on_device(): pl.pallas_call(functools.partial(kernel, (moms, energies, modes, orbitals...  25.2 us
    unnamed x1, local copies, waits for them, and re-layouts  0.71 us

profile of v8, /device:TPU:0, one launch (start us, length us, event | category | flops | bytes accessed | tf_op | source)
XLA Modules:
  0.0 25.9 jit_solution(11937801614551860800)
XLA Ops:
  0.0 25.2 %shard_map.55 = f32[1,1,8,64,128]{4,3,2,1,0:T(8,128)S(1)} custom-call(f32[1,1,8,64,128]{4,3,2,1,0:T(8,128)} %green_hbm.1, bf16[32,3,64,64]{3,2,1,0:T(8,128)(2,1)} %couplings_hbm.1, s32[2,8]{1,0:T(2,128)} %bitcast.3, s32[3]{0:T(128)} %shift_idx_hbm.1, f32[3,2,4]{2,1,0:T(2,128)} %bitcast.2), custom_call_target="tpu_custom_call" | custom-call | tf_op jit(solution)/shard_map/pallas_call | solution.py:289
  25.2 0.7 %copy.7 = f32[1,1,8,64,128]{4,3,2,1,0:T(8,128)} copy(f32[1,1,8,64,128]{4,3,2,1,0:T(8,128)S(1)} %shard_map.55) | data formatting | bytes 524288

commit v9 on v7

--- a/solution.py
+++ b/solution.py
@@ -62,6 +62,15 @@
 
     load_green = pltpu.make_async_copy(green_hbm, green, load_sem.at[0])
     load_green.start()
+    edge = jnp.zeros((SHIFT_MAX, rows, lanes), jnp.float32)
+    for source in range(HALVES):
+        held[source, pl.ds(0, SHIFT_MAX)] = edge
+        held[source, pl.ds(SHIFT_MAX + energies, SHIFT_MAX)] = edge
+        for side in range(1, cores):
+            aside[side - 1, source, pl.ds(0, SHIFT_MAX)] = edge
+            aside[side - 1, source, pl.ds(SHIFT_MAX + energies, SHIFT_MAX)] = edge
+
+    load_green.wait()
     load_couplings = pltpu.make_async_copy(couplings_hbm, couplings, load_sem.at[1])
     load_couplings.start()
     load_small = [
@@ -71,16 +80,6 @@
     ]
     for load in load_small:
         load.start()
-
-    edge = jnp.zeros((SHIFT_MAX, rows, lanes), jnp.float32)
-    for source in range(HALVES):
-        held[source, pl.ds(0, SHIFT_MAX)] = edge
-        held[source, pl.ds(SHIFT_MAX + energies, SHIFT_MAX)] = edge
-        for side in range(1, cores):
-            aside[side - 1, source, pl.ds(0, SHIFT_MAX)] = edge
-            aside[side - 1, source, pl.ds(SHIFT_MAX + energies, SHIFT_MAX)] = edge
-
-    load_green.wait()
     mask = left_lanes((rows, lanes))
     for pair in range(energies):
         top = green[0, 0, pair, pl.ds(0, rows), :]
@@ -206,11 +205,11 @@
             device_id_type=MESH,
         )
 
-    place = lax.rem(here, reach)
+    upper = here // reach
 
     def one_group(index, carry):
         chosen = [
-            around(here // reach, 1 - side, 2) * reach + lax.rem(place + index + side, reach) for side in range(group)
+            upper * (group * index + member) + (1 - upper) * (index + member * reach) for member in range(group)
         ]
         sums = [[] for _ in range(modes)]
         for energy in chosen:

time: 23.4 us -> 23.4 us (level)
  the two profiles are of different devices: /device:TPU:0 before, /device:TPU:11 now
where the time goes in v9:
time: 23.4 us; the launch traced here: 23.3 us
  Pallas kernels  22.6 us (97%)
  local copies, waits for them, and re-layouts  0.71 us (3%)
    pallas_call x1, Pallas kernels, on_device(): pl.pallas_call(functools.partial(kernel, (moms, energies, modes, orbitals...  22.6 us
    unnamed x1, local copies, waits for them, and re-layouts  0.71 us

profile of v9, /device:TPU:11, one launch (start us, length us, event | category | flops | bytes accessed | tf_op | source)
XLA Modules:
  0.0 23.3 jit_solution(3332300470396549082)
XLA Ops:
  0.0 22.6 %shard_map.55 = f32[1,1,8,64,128]{4,3,2,1,0:T(8,128)S(1)} custom-call(f32[1,1,8,64,128]{4,3,2,1,0:T(8,128)} %green_hbm.1, bf16[32,3,64,64]{3,2,1,0:T(8,128)(2,1)} %couplings_hbm.1, s32[2,8]{1,0:T(2,128)} %bitcast.3, s32[3]{0:T(128)} %shift_idx_hbm.1, f32[3,2,4]{2,1,0:T(2,128)} %bitcast.2), custom_call_target="tpu_custom_call" | custom-call | tf_op jit(solution)/shard_map/pallas_call | solution.py:284
  22.6 0.7 %copy.7 = f32[1,1,8,64,128]{4,3,2,1,0:T(8,128)} copy(f32[1,1,8,64,128]{4,3,2,1,0:T(8,128)S(1)} %shard_map.55) | data formatting | bytes 524288

commit v10 on v8

--- a/solution.py
+++ b/solution.py
@@ -133,13 +133,9 @@
     far_first = sorted(range(energies), key=lambda step: -min(step, energies - step))
     slots = [(turn, step) for step in far_first for turn in range(HALVES)]
     near_first = slots[::-1]
-    place = lax.rem(here, reach)
-    for index in range(reach):
-        for side in range(2):
-            to = around(here // reach, 1 - side, 2) * reach + lax.rem(place + index + side, reach)
-            for turn in range(HALVES):
-                if (turn, side, index) != (0, 1, reach - 1):
-                    send_in(turn, lax.rem(to - here + energies, energies)).start()
+    remote = [slot for slot in slots if slot != (0, 0)]
+    for turn, step in remote:
+        send_in(turn, step).start()
 
     held[half, SHIFT_MAX + here] = packed[half, here]
 
@@ -212,9 +208,11 @@
             device_id_type=MESH,
         )
 
+    upper = here // reach
+
     def one_group(index, carry):
         chosen = [
-            around(here // reach, 1 - side, 2) * reach + lax.rem(place + index + side, reach) for side in range(group)
+            upper * (group * index + member) + (1 - upper) * (index + member * reach) for member in range(group)
         ]
         sums = [[] for _ in range(modes)]
         for energy in chosen:

time: 26 us -> 23.6 us (0.908)
  the two profiles are of different devices: /device:TPU:0 before, /device:TPU:11 now
where the time goes in v10:
time: 23.6 us; the launch traced here: 23.4 us
  Pallas kernels  22.7 us (96%)
  local copies, waits for them, and re-layouts  0.71 us (3%)
    pallas_call x1, Pallas kernels, on_device(): pl.pallas_call(functools.partial(kernel, (moms, energies, modes, orbitals...  22.7 us
    unnamed x1, local copies, waits for them, and re-layouts  0.71 us

profile of v10, /device:TPU:11, one launch (start us, length us, event | category | flops | bytes accessed | tf_op | source)
XLA Modules:
  0.0 23.4 jit_solution(12397796817255894943)
XLA Ops:
  0.0 22.7 %shard_map.55 = f32[1,1,8,64,128]{4,3,2,1,0:T(8,128)S(1)} custom-call(f32[1,1,8,64,128]{4,3,2,1,0:T(8,128)} %green_hbm.1, bf16[32,3,64,64]{3,2,1,0:T(8,128)(2,1)} %couplings_hbm.1, s32[2,8]{1,0:T(2,128)} %bitcast.3, s32[3]{0:T(128)} %shift_idx_hbm.1, f32[3,2,4]{2,1,0:T(2,128)} %bitcast.2), custom_call_target="tpu_custom_call" | custom-call | tf_op jit(solution)/shard_map/pallas_call | solution.py:287
  22.7 0.7 %copy.7 = f32[1,1,8,64,128]{4,3,2,1,0:T(8,128)} copy(f32[1,1,8,64,128]{4,3,2,1,0:T(8,128)S(1)} %shard_map.55) | data formatting | bytes 524288

commit v11 on v9

--- a/solution.py
+++ b/solution.py
@@ -208,9 +208,11 @@
     upper = here // reach
 
     def one_group(index, carry):
-        chosen = [
-            upper * (group * index + member) + (1 - upper) * (index + member * reach) for member in range(group)
-        ]
+        chosen = []
+        for member in range(group):
+            spot = upper * (group * index + member) + (1 - upper) * (index + member * reach)
+            late = (spot % reach >= reach // 2).astype(jnp.int32)
+            chosen.append(spot + late * (1 - 2 * (spot % 2)))
         sums = [[] for _ in range(modes)]
         for energy in chosen:
             for mode in range(modes):

time: 23.4 us -> 23.3 us (level)
  the two profiles are of different devices: /device:TPU:11 before, /device:TPU:9 now
where the time goes in v11:
time: 23.3 us; the launch traced here: 23.2 us
  Pallas kernels  22.5 us (97%)
  local copies, waits for them, and re-layouts  0.71 us (3%)
    pallas_call x1, Pallas kernels, on_device(): pl.pallas_call(functools.partial(kernel, (moms, energies, modes, orbitals...  22.5 us
    unnamed x1, local copies, waits for them, and re-layouts  0.71 us

profile of v11, /device:TPU:9, one launch (start us, length us, event | category | flops | bytes accessed | tf_op | source)
XLA Modules:
  0.0 23.2 jit_solution(17495701768333533770)
XLA Ops:
  0.0 22.5 %shard_map.55 = f32[1,1,8,64,128]{4,3,2,1,0:T(8,128)S(1)} custom-call(f32[1,1,8,64,128]{4,3,2,1,0:T(8,128)} %green_hbm.1, bf16[32,3,64,64]{3,2,1,0:T(8,128)(2,1)} %couplings_hbm.1, s32[2,8]{1,0:T(2,128)} %bitcast.3, s32[3]{0:T(128)} %shift_idx_hbm.1, f32[3,2,4]{2,1,0:T(2,128)} %bitcast.2), custom_call_target="tpu_custom_call" | custom-call | tf_op jit(solution)/shard_map/pallas_call | solution.py:286
  22.5 0.7 %copy.7 = f32[1,1,8,64,128]{4,3,2,1,0:T(8,128)} copy(f32[1,1,8,64,128]{4,3,2,1,0:T(8,128)S(1)} %shard_map.55) | data formatting | bytes 524288
